TPU v7x, 256 devices: a whole 4x4x8 slice. The times are simulated.
256 devices in a mesh: prefix: 16 (over y, z_lo), resp: 16 (over z_hi, x, core).
Axes of the slice: x: 4, y: 4, z: 8 (z_hi: 2, z_lo: 4; z = z_hi * 4 + z_lo), core: 2. Of those that a mesh axis runs over, the one named last changes fastest.
Arguments:
- response_queries: bfloat16 [16, 2048, 2560], P('resp', 'prefix'), may hold values from -120 to 120
- response_keys: bfloat16 [16, 2048, 512], P('resp', 'prefix'), may hold values from -6 to 6
- response_values: bfloat16 [16, 2048, 512], P('resp', 'prefix'), may hold values from -6 to 6
- prompt_keys: bfloat16 [768, 512], P('prefix'), may hold values from -6.1 to 6.1
- prompt_values: bfloat16 [768, 512], P('prefix'), may hold values from -6 to 6
- output_grad: bfloat16 [16, 2048, 2560], P('resp', 'prefix'), may hold values from -6 to 6
- lengths: int32 [16], replicated, may hold values from 1 to 2048, 17408 in all
Outputs:
- attention_out: bfloat16 [16, 2048, 2560], P('resp', 'prefix')
- query_grad: bfloat16 [16, 2048, 2560], P('resp', 'prefix')
- response_key_grad: float32 [16, 2048, 512], P('resp', 'prefix')
- response_value_grad: float32 [16, 2048, 512], P('resp', 'prefix')
- prompt_key_grad: float32 [768, 512], P('prefix')
- prompt_value_grad: float32 [768, 512], P('prefix')
Inputs may be any that keep to these rules, and one draw needn't show every extreme that they name: `lengths`: the longest response has exactly 2048 positions.
All inputs are finite; a program needn't handle non-finite values.
Results may differ from a plain program's by a relative error of at most 0.035.
Values may be sent and summed in bfloat16 or wider, within the bound.
No kernel may reach another device: no remote copies, remote signals or barrier semaphores. Data moves between devices by JAX's collectives and lax.ppermute only.
A program may use at most 128 MiB of HBM per device.

v0:
```python
import math

import jax
import jax.numpy as jnp
from jax import lax
from jax.experimental import pallas as pl
from jax.experimental.pallas import tpu as pltpu
from jax.sharding import PartitionSpec as P

HD = 128
BLOCK = 128
PROMPT_ROWS = 48
PIECE = PROMPT_ROWS + BLOCK
HEADS = 5
NY = 4
NZ = 4
PROMPT = PROMPT_ROWS * NY * NZ
KEYS = PROMPT + BLOCK * NY * NZ
ROWS = NY * HEADS * BLOCK
CHUNK = 256
TILE = 256
MASKED = -1e30
SCALE = 1.0 / math.sqrt(HD)
SCALE2 = SCALE * math.log2(math.e)
F32 = jnp.float32
BF16 = jnp.bfloat16
CLASSES = ((0, 2, 2, 0), (2, 5, 4, 0), (5, 7, 6, 4), (7, 10, 8, 4))
TILES = ROWS // TILE
RESP = KEYS - PROMPT
GROUP = HEADS * BLOCK
VMEM = pl.BlockSpec(memory_space=pltpu.VMEM)
SMEM = pl.BlockSpec(memory_space=pltpu.SMEM)


def shaped(shape, dtype):
    return jax.ShapeDtypeStruct(shape, dtype)


def aligned(start, size):
    return pl.ds(pl.multiple_of(start, size), size)


def head_rows(block):
    return aligned(lax.rem(block, NY) * GROUP, GROUP)


def tile_positions(tile, z):
    u = tile * 2
    lane = lax.broadcasted_iota(jnp.int32, (1, TILE), 1)
    low = (u // HEADS * NZ + z) * BLOCK
    high = ((u + 1) // HEADS * NZ + z) * BLOCK - BLOCK
    return lane + jnp.where(lane < BLOCK, low, high)


def causal(s, chunks, first_masked, query_pos):
    end, start = chunks * CHUNK, first_masked * CHUNK
    key_pos = lax.broadcasted_iota(jnp.int32, (end - start, TILE), 0) + start
    last = jnp.where(key_pos <= query_pos, s[start:], MASKED)
    return jnp.concatenate([s[:start], last]) if start else last


def over_tiles(z, length, body, skip):
    for first, last, chunks, first_masked in CLASSES:

        def step(tile, carry, chunks=chunks, first_masked=first_masked):
            active = (tile * 2 // HEADS * NZ + z) * BLOCK < length

            @pl.when(active)
            def _():
                body(tile, chunks, first_masked)

            @pl.when(jnp.logical_not(active))
            def _():
                skip(tile)

            return carry

        lax.fori_loop(first, last, step, 0)


def attend_kernel(
    info,
    x0, x1, x2, x3,
    kv0, kv1, kv2, kv3,
    p0, p1, p2, p3,
    d0, d1, d2, d3,
    r0, r1, r2, r3,
    qs, gs, ks, vs, kt, vt, kp, vp, kpt, vpt, dk, dv, dkp, dvp, os, dq, sent, sems,
):
    y = info[0]
    z = info[1]
    length = info[2]
    for s, x in enumerate((x0, x1, x2, x3)):
        block = lax.rem(y - s + NY, NY)
        start = (block * NZ + z) * BLOCK
        valid = (lax.broadcasted_iota(jnp.int32, (BLOCK, HD), 0) + start) < length
        for j in range(HEADS):
            at = aligned((block * HEADS + j) * BLOCK, BLOCK)
            cols = slice(j * HD, (j + 1) * HD)
            qs[at, :] = x[0, :, cols]
            gs[at, :] = jnp.where(valid, x[1, :, cols].astype(F32), 0.0).astype(BF16)
    for s, kv in enumerate((kv0, kv1, kv2, kv3)):
        zp = lax.rem(z - s + NZ, NZ)
        for b in range(NY):
            at = aligned((zp * NY + b) * PROMPT_ROWS, PROMPT_ROWS)
            kp[at, :] = kv[b, 0, :PROMPT_ROWS, :]
            vp[at, :] = kv[b, 1, :PROMPT_ROWS, :]
            at = aligned((b * NZ + zp) * BLOCK, BLOCK)
            k = kv[b, 0, PROMPT_ROWS:, :]
            v = kv[b, 1, PROMPT_ROWS:, :]
            ks[at, :] = k
            vs[at, :] = v
            kt[:, at] = k.T
            vt[:, at] = v.T
    for c in range(PROMPT // BLOCK):
        rows = slice(c * BLOCK, (c + 1) * BLOCK)
        kpt[:, rows] = kp[rows, :].T
        vpt[:, rows] = vp[rows, :].T
    for grad in (dk, dv, dkp, dvp):
        grad[...] = jnp.zeros_like(grad)

    def tile_step(tile, chunks, first_masked):
        at = aligned(tile * TILE, TILE)
        query_pos = tile_positions(tile, z)
        q = qs[at, :]
        qt = q.T
        n = chunks * CHUNK
        first = jnp.dot(kp[...], qt, preferred_element_type=F32)
        s = jnp.dot(ks[:n, :], qt, preferred_element_type=F32)
        s = causal(s, chunks, first_masked, query_pos)
        top = jnp.maximum(
            jnp.max(first, axis=0, keepdims=True), jnp.max(s, axis=0, keepdims=True)
        )
        first = jnp.exp2((first - top) * SCALE2)
        total = jnp.sum(first, axis=0, keepdims=True)
        first = first.astype(BF16)
        out_t = jnp.dot(vpt[...], first, preferred_element_type=F32)
        p = jnp.exp2((s - top) * SCALE2)
        total = total + jnp.sum(p, axis=0, keepdims=True)
        p = p.astype(BF16)
        out_t = out_t + jnp.dot(vt[:, :n], p, preferred_element_type=F32)
        inv = 1.0 / total
        out_t = out_t * inv
        os[at, :] = jnp.where(query_pos < length, out_t, 0.0).T.astype(BF16)
        grad_t = gs[at, :].astype(F32).T
        delta = jnp.sum(grad_t * out_t, axis=0, keepdims=True) * inv
        grad_t = grad_t * inv
        grad = grad_t.T.astype(BF16)
        grad_t = grad_t.astype(BF16)
        dp = jnp.dot(vp[...], grad_t, preferred_element_type=F32)
        ds = (first.astype(F32) * (dp - delta)).astype(BF16)
        dvp[...] += jnp.dot(first, grad, preferred_element_type=F32)
        dkp[...] += jnp.dot(ds, q, preferred_element_type=F32)
        dq_t = jnp.dot(kpt[...], ds, preferred_element_type=F32)
        dp = jnp.dot(vs[:n, :], grad_t, preferred_element_type=F32)
        ds = (p.astype(F32) * (dp - delta)).astype(BF16)
        dv[:n, :] += jnp.dot(p, grad, preferred_element_type=F32)
        dk[:n, :] += jnp.dot(ds, q, preferred_element_type=F32)
        dq_t = dq_t + jnp.dot(kt[:, :n], ds, preferred_element_type=F32)
        dq[at, :] = (dq_t * SCALE).T.astype(BF16)

    def skip(tile):
        at = aligned(tile * TILE, TILE)
        os[at, :] = jnp.zeros((TILE, HD), BF16)
        dq[at, :] = jnp.zeros((TILE, HD), BF16)

    over_tiles(z, length, tile_step, skip)
    copies = []
    for s, r in enumerate((r0, r1, r2, r3)):
        zp = lax.rem(z + s, NZ)
        for b in range(NY):
            at = aligned((b * NZ + zp) * BLOCK, BLOCK)
            sent[s, b, 0] = (dk[at, :] * SCALE).astype(BF16)
            sent[s, b, 1] = dv[at, :].astype(BF16)
        copies.append(pltpu.make_async_copy(sent.at[s], r, sems.at[s]))
        copies[-1].start()
    for s, d in enumerate((d0, d1, d2, d3)):
        d[:GROUP, :] = os[head_rows(y + s), :]
        d[GROUP:, :] = dq[head_rows(y + s), :]
    for s, p in enumerate((p0, p1, p2, p3)):
        zp = lax.rem(z + s, NZ)
        for b in range(NY):
            at = aligned((zp * NY + b) * PROMPT_ROWS, PROMPT_ROWS)
            p[b, 0] = (dkp[at, :] * SCALE).astype(BF16)
            p[b, 1] = dvp[at, :].astype(BF16)
    for copy in copies:
        copy.wait()


def attend(info, rows, keyvals):
    return pl.pallas_call(
        attend_kernel,
        out_shape=[shaped((NY, 2, PROMPT_ROWS, HD), BF16)] * NZ
        + [shaped((2 * GROUP, HD), BF16)] * NY
        + [shaped((NY, 2, BLOCK, HD), BF16)] * NZ,
        in_specs=[SMEM] + [VMEM] * 8,
        out_specs=[VMEM] * 8 + [pl.BlockSpec(memory_space=pl.ANY)] * NZ,
        scratch_shapes=[pltpu.VMEM((ROWS, HD), BF16)] * 2
        + [pltpu.VMEM((RESP, HD), BF16)] * 2
        + [pltpu.VMEM((HD, RESP), BF16)] * 2
        + [pltpu.VMEM((PROMPT, HD), BF16)] * 2
        + [pltpu.VMEM((HD, PROMPT), BF16)] * 2
        + [pltpu.VMEM((RESP, HD), F32)] * 2
        + [pltpu.VMEM((PROMPT, HD), F32)] * 2
        + [pltpu.VMEM((ROWS, HD), BF16)] * 2
        + [pltpu.VMEM((NZ, NY, 2, BLOCK, HD), BF16), pltpu.SemaphoreType.DMA((NZ,))],
        compiler_params=pltpu.CompilerParams(vmem_limit_bytes=48 * 2**20),
        name="attend",
    )(info, *rows, *keyvals)


def settle_kernel(
    info, r0, r1, r2, r3, prompt, p0, p1, p2, p3
):
    y = info[0]
    for s, p in enumerate((p0, p1, p2, p3)):
        b = lax.rem(y + s, NY)
        for i in range(2):
            p[i * PIECE : i * PIECE + PROMPT_ROWS, :] = prompt[b, i].astype(BF16)
            p[i * PIECE + PROMPT_ROWS : (i + 1) * PIECE, :] = (
                (r0[b, i].astype(F32) + r1[b, i].astype(F32))
                + (r2[b, i].astype(F32) + r3[b, i].astype(F32))
            ).astype(BF16)


def settle(info, terms, prompt):
    return pl.pallas_call(
        settle_kernel,
        out_shape=[shaped((2 * PIECE, HD), BF16)] * NY,
        in_specs=[SMEM] + [VMEM] * 5,
        out_specs=[VMEM] * 4,
        compiler_params=pltpu.CompilerParams(vmem_limit_bytes=16 * 2**20),
        name="settle",
    )(info, *terms, prompt)


def rows_kernel(info, d0, d1, d2, d3, att, dq):
    y = info[0]
    for s, d in enumerate((d0, d1, d2, d3)):
        block = lax.rem(y - s + NY, NY)
        for j in range(HEADS):
            at = aligned((block * HEADS + j) * HD, HD)
            att[:, at] = d[j * BLOCK : (j + 1) * BLOCK, :]
            dq[:, at] = d[GROUP + j * BLOCK : GROUP + (j + 1) * BLOCK, :]


def lay_rows(info, pieces):
    return pl.pallas_call(
        rows_kernel,
        out_shape=[shaped((BLOCK, NY * HEADS * HD), BF16)] * 2,
        in_specs=[SMEM] + [VMEM] * 4,
        out_specs=[VMEM] * 2,
        compiler_params=pltpu.CompilerParams(vmem_limit_bytes=16 * 2**20),
        name="lay_rows",
    )(info, *pieces)


def place_kernel(info, done, p0, p1, p2, p3, dk, dv, pk, pv):
    y = info[0]
    for s, p in enumerate((p0, p1, p2, p3)):
        at = aligned(lax.rem(y - s + NY, NY) * HD, HD)
        pk[:, at] = p[:PROMPT_ROWS, :].astype(F32)
        dk[:, at] = p[PROMPT_ROWS:PIECE, :].astype(F32)
        pv[:, at] = p[PIECE : PIECE + PROMPT_ROWS, :].astype(F32)
        dv[:, at] = p[PIECE + PROMPT_ROWS : 2 * PIECE, :].astype(F32)


def place(info, done, pieces):
    out = shaped((BLOCK, NY * HD), F32)
    prompt_out = shaped((PROMPT_ROWS, NY * HD), F32)
    return pl.pallas_call(
        place_kernel,
        out_shape=[out, out, prompt_out, prompt_out],
        in_specs=[SMEM, pl.BlockSpec(memory_space=pl.ANY)] + [VMEM] * 4,
        out_specs=[VMEM] * 4,
        compiler_params=pltpu.CompilerParams(vmem_limit_bytes=16 * 2**20),
        name="place",
    )(info, done, *pieces)


def y_shift(a, s):
    pairs = [(i * NZ + k, (i + s) % NY * NZ + k) for i in range(NY) for k in range(NZ)]
    return lax.ppermute(a, "prefix", pairs)


def z_shift(a, s):
    pairs = [(i * NZ + k, i * NZ + (k + s) % NZ) for i in range(NY) for k in range(NZ)]
    return lax.ppermute(a, "prefix", pairs)


def core_swap(a):
    return lax.ppermute(a, "resp", [(i, i ^ 1) for i in range(16)])


def x_swap(a, bit):
    return lax.ppermute(a, "resp", [(i, i ^ (2 * bit)) for i in range(16)])


def far_swap(a):
    return lax.ppermute(a, "resp", [(i, i ^ 8) for i in range(16)])


def over_responses(terms):
    core = lax.axis_index("resp") % 2
    dk, dv = terms[0], terms[1]
    half = jnp.where(core == 0, dk, dv) + core_swap(jnp.where(core == 0, dv, dk))
    for swap in (lambda a: x_swap(a, 1), lambda a: x_swap(a, 2), far_swap):
        low = half.astype(BF16)
        half = low.astype(F32) + swap(low).astype(F32)
    other = core_swap(half.astype(BF16)).astype(F32)
    half = half.astype(BF16).astype(F32)
    return jnp.stack([jnp.where(core == 0, half, other), jnp.where(core == 0, other, half)])


def by_y(pieces):
    return [pieces[0]] + [y_shift(pieces[s], s) for s in range(1, NY)]


def by_z(pieces):
    return [pieces[0]] + [z_shift(pieces[s], s) for s in range(1, NZ)]


def per_device(
    response_queries,
    response_keys,
    response_values,
    prompt_keys,
    prompt_values,
    output_grad,
    lengths,
):
    prefix = lax.axis_index("prefix")
    y, z = prefix // NZ, prefix % NZ
    info = jnp.stack([y, z, lengths[lax.axis_index("resp")]]).astype(jnp.int32)
    pick = lax.dynamic_index_in_dim

    def split(a, width):
        return [
            lax.dynamic_slice_in_dim(a, (y + s) % NY * width, width, a.ndim - 1)
            for s in range(NY)
        ]

    keyvals = jnp.stack(
        [
            jnp.concatenate([prompt_keys, response_keys[0]], axis=0),
            jnp.concatenate([prompt_values, response_values[0]], axis=0),
        ]
    )
    keyvals = by_y(split(keyvals, HD))
    *keyvals, queries, grads = lax.optimization_barrier(
        (*keyvals, response_queries[0], output_grad[0])
    )
    stacked = jnp.stack(keyvals)
    keyvals = jnp.stack([pick(stacked, (y - b) % NY, 0, keepdims=False) for b in range(NY)])
    keyvals = by_z([keyvals] * NZ)
    rows = by_y(split(jnp.stack([queries, grads]), HEADS * HD))

    results = attend(info, rows, keyvals)
    prompt_terms = by_z(results[:4])
    d0, d1, d2, d3 = results[4:8]
    d1, d3 = y_shift(d1, 1), y_shift(d3, 3)
    *prompt_terms, d1, d3, d2, t1, t2, t3 = lax.optimization_barrier(
        (*prompt_terms, d1, d3, d2, *results[9:])
    )
    prompt = sum(t.astype(F32) for t in prompt_terms)
    prompt = prompt.transpose(1, 0, 2, 3).reshape(2, NY * PROMPT_ROWS, HD)
    once = jnp.minimum(lengths[0], 1)
    terms = by_z([results[8], t1, t2, t3])
    d2 = y_shift(d2, 2)
    prompt = lax.fori_loop(0, once, lambda i, terms: over_responses(terms), prompt)
    prompt = prompt.reshape(2, NY, PROMPT_ROWS, HD).transpose(1, 0, 2, 3)
    pieces = settle(info, terms, prompt)
    d2, *pieces = lax.optimization_barrier((d2, *pieces))
    attention_out, query_grad = lay_rows(info, (d0, d1, d2, d3))
    key_own, value_own, prompt_key_grad, prompt_value_grad = place(
        info, query_grad, by_y(pieces)
    )
    return (
        attention_out[None],
        query_grad[None],
        key_own[None],
        value_own[None],
        prompt_key_grad,
        prompt_value_grad,
    )


def solution(mesh):
    return jax.shard_map(
        per_device,
        mesh=mesh,
        in_specs=(
            P("resp", "prefix", None),
            P("resp", "prefix", None),
            P("resp", "prefix", None),
            P("prefix", None),
            P("prefix", None),
            P("resp", "prefix", None),
            P(),
        ),
        out_specs=(
            P("resp", "prefix", None),
            P("resp", "prefix", None),
            P("resp", "prefix", None),
            P("resp", "prefix", None),
            P("prefix", None),
            P("prefix", None),
        ),
        check_vma=False,
    )
```

profile of v0, /device:TPU:1, one launch (start us, length us, event | category | flops | bytes accessed | tf_op | source)
XLA Modules:
  0.0 129.3 jit_solution(10654153385151504222)
XLA Ops:
  0.8 1.1 maximum_bitcast_fusion
  2.0 2.2 %collective-permute-start.5 = (bf16[2,176,128]{2,1,0:T(8,128)(2,1)S(1)}, bf16[2,176,128]{2,1,0:T(8,128)(2,1)S(1)}, u32[]{:S(2)}, u32[]{:S(2)}) collective-permute-start(bf16[2,176,128]{2,1,0:T(8,128)(2,1)S(1)} %get-tuple-element.156), channel_id=1, source_target_pairs={{0,64},{16,80},{32,96},{48,112},{64,128},{80,144},{96,160},{112,17... | collective-permute-start | bytes 270344 | tf_op jit(solution)/shard_map/ppermute | solution.py:283
  4.2 2.6 %collective-permute-start.6 = (bf16[2,176,128]{2,1,0:T(8,128)(2,1)S(1)}, bf16[2,176,128]{2,1,0:T(8,128)(2,1)S(1)}, u32[]{:S(2)}, u32[]{:S(2)}) collective-permute-start(bf16[2,176,128]{2,1,0:T(8,128)(2,1)S(1)} %get-tuple-element.157), channel_id=1, source_target_pairs={{0,128},{16,144},{32,160},{48,176},{64,192},{80,208},{96,224},{112... | collective-permute-start | bytes 270344 | tf_op jit(solution)/shard_map/ppermute | solution.py:283
  6.8 1.1 collective-permute-start.7
  7.9 2.6 %collective-permute-done.6 = bf16[2,176,128]{2,1,0:T(8,128)(2,1)S(1)} collective-permute-done((bf16[2,176,128]{2,1,0:T(8,128)(2,1)S(1)}, bf16[2,176,128]{2,1,0:T(8,128)(2,1)S(1)}, u32[]{:S(2)}, u32[]{:S(2)}) %collective-permute-start.6) | collective-permute-done | bytes 90144 | tf_op jit(solution)/shard_map/ppermute | solution.py:283
  10.5 0.9 fusion.3
  11.4 2.0 %collective-permute-start.10 = (bf16[2,128,640]{2,1,0:T(8,128)(2,1)S(1)}, bf16[2,128,640]{2,1,0:T(8,128)(2,1)S(1)}, u32[]{:S(2)}, u32[]{:S(2)}) collective-permute-start(bf16[2,128,640]{2,1,0:T(8,128)(2,1)S(1)} %get-tuple-element.146), channel_id=1, source_target_pairs={{0,192},{16,208},{32,224},{48,240},{64,0},{80,16},{96,32},{112,48}... | collective-permute-start | bytes 983048 | tf_op jit(solution)/shard_map/ppermute | solution.py:283
  13.6 2.1 %collective-permute-start.11 = (bf16[4,2,176,128]{3,2,1,0:T(8,128)(2,1)S(1)}, bf16[4,2,176,128]{3,2,1,0:T(8,128)(2,1)S(1)}, u32[]{:S(2)}, u32[]{:S(2)}) collective-permute-start(bf16[4,2,176,128]{3,2,1,0:T(8,128)(2,1)S(1)} %pad_maximum_fusion.2.kv0), channel_id=1, source_target_pairs={{0,16},{16,32},{32,48},{48,0},{64,80},{80,96},{96,112},{112,64},{1... | collective-permute-start | bytes 1081352 | tf_op jit(solution)/shard_map/ppermute | solution.py:288
  15.6 3.0 %collective-permute-start.12 = (bf16[4,2,176,128]{3,2,1,0:T(8,128)(2,1)S(1)}, bf16[4,2,176,128]{3,2,1,0:T(8,128)(2,1)S(1)}, u32[]{:S(2)}, u32[]{:S(2)}) collective-permute-start(bf16[4,2,176,128]{3,2,1,0:T(8,128)(2,1)S(1)} %pad_maximum_fusion.2.kv0), channel_id=1, source_target_pairs={{0,32},{16,48},{32,0},{48,16},{64,96},{80,112},{96,64},{112,80},{1... | collective-permute-start | bytes 1081352 | tf_op jit(solution)/shard_map/ppermute | solution.py:288
  18.6 0.7 collective-permute-start.13
  19.4 1.5 %collective-permute-start.9 = (bf16[2,128,640]{2,1,0:T(8,128)(2,1)}, bf16[2,128,640]{2,1,0:T(8,128)(2,1)S(1)}, u32[]{:S(2)}, u32[]{:S(2)}) collective-permute-start(bf16[2,128,640]{2,1,0:T(8,128)(2,1)} %get-tuple-element.149), channel_id=1, source_target_pairs={{0,128},{16,144},{32,160},{48,176},{64,192},{80,208},{96,224},{112... | collective-permute-start | bytes 983048 | tf_op jit(solution)/shard_map/ppermute | solution.py:283
  20.8 0.6 fusion.11
  21.4 0.7 pad_add_fusion.info
  22.1 7.3 %collective-permute-done.8.x1 = bf16[2,128,640]{2,1,0:T(8,128)(2,1)S(1)} collective-permute-done((bf16[2,128,640]{2,1,0:T(8,128)(2,1)}, bf16[2,128,640]{2,1,0:T(8,128)(2,1)S(1)}, u32[]{:S(2)}, u32[]{:S(2)}) %collective-permute-start.8) | collective-permute-done | bytes 327712 | tf_op jit(solution)/shard_map/ppermute | solution.py:283
  29.5 2.9 %collective-permute-done.9.x2 = bf16[2,128,640]{2,1,0:T(8,128)(2,1)S(1)} collective-permute-done((bf16[2,128,640]{2,1,0:T(8,128)(2,1)}, bf16[2,128,640]{2,1,0:T(8,128)(2,1)S(1)}, u32[]{:S(2)}, u32[]{:S(2)}) %collective-permute-start.9) | collective-permute-done | bytes 327712 | tf_op jit(solution)/shard_map/ppermute | solution.py:283
  32.4 10.3 %collective-permute-done.12.kv2 = bf16[4,2,176,128]{3,2,1,0:T(8,128)(2,1)S(1)} collective-permute-done((bf16[4,2,176,128]{3,2,1,0:T(8,128)(2,1)S(1)}, bf16[4,2,176,128]{3,2,1,0:T(8,128)(2,1)S(1)}, u32[]{:S(2)}, u32[]{:S(2)}) %collective-permute-start.12) | collective-permute-done | bytes 360480 | tf_op jit(solution)/shard_map/ppermute | solution.py:288
  42.7 26.5 %attend.1 = (bf16[4,2,48,128]{3,2,1,0:T(8,128)(2,1)S(1)}, bf16[4,2,48,128]{3,2,1,0:T(8,128)(2,1)}, bf16[4,2,48,128]{3,2,1,0:T(8,128)(2,1)}, bf16[4,2,48,128]{3,2...) custom-call(s32[3]{0:T(128)S(1)} %pad_add_fusion.info, ...), custom_call_target="tpu_custom_call" | custom-call | tf_op jit(solution)/shard_map/attend/pallas_call | solution.py:191
  69.2 0.7 copy-done.1
  69.9 0.7 copy-done.3
  70.6 0.7 copy-done.5
  71.3 0.7 copy-done.7
  72.0 2.7 %collective-permute-start.18 = (bf16[1280,128]{1,0:T(8,128)(2,1)}, bf16[1280,128]{1,0:T(8,128)(2,1)S(1)}, u32[]{:S(2)}, u32[]{:S(2)}) collective-permute-start(bf16[1280,128]{1,0:T(8,128)(2,1)} %get-tuple-element.106), channel_id=1, source_target_pairs={{0,192},{16,208},{32,224},{48,240},{64,0},{80,16},{96,32},{112,48}... | collective-permute-start | bytes 983048 | tf_op jit(solution)/shard_map/ppermute | solution.py:283
  74.7 8.0 %collective-permute-start.14 = (bf16[4,2,48,128]{3,2,1,0:T(8,128)(2,1)}, bf16[4,2,48,128]{3,2,1,0:T(8,128)(2,1)S(1)}, u32[]{:S(2)}, u32[]{:S(2)}) collective-permute-start(bf16[4,2,48,128]{3,2,1,0:T(8,128)(2,1)} %get-tuple-element.102), channel_id=1, source_target_pairs={{0,16},{16,32},{32,48},{48,0},{64,80},{80,96},{96,112},{112,64},{1... | collective-permute-start | bytes 294920 | tf_op jit(solution)/shard_map/ppermute | solution.py:288
  82.7 2.1 %collective-permute-start.16 = (bf16[4,2,48,128]{3,2,1,0:T(8,128)(2,1)S(1)}, bf16[4,2,48,128]{3,2,1,0:T(8,128)(2,1)S(1)}, u32[]{:S(2)}, u32[]{:S(2)}) collective-permute-start(bf16[4,2,48,128]{3,2,1,0:T(8,128)(2,1)S(1)} %get-tuple-element.104), channel_id=1, source_target_pairs={{0,48},{16,0},{32,16},{48,32},{64,112},{80,64},{96,80},{112,96},{1... | collective-permute-start | bytes 294920 | tf_op jit(solution)/shard_map/ppermute | solution.py:288
  85.3 0.4 collective-permute-done.14
  85.7 5.5 %collective-permute-done.15 = bf16[4,2,48,128]{3,2,1,0:T(8,128)(2,1)S(1)} collective-permute-done((bf16[4,2,48,128]{3,2,1,0:T(8,128)(2,1)}, bf16[4,2,48,128]{3,2,1,0:T(8,128)(2,1)S(1)}, u32[]{:S(2)}, u32[]{:S(2)}) %collective-permute-start.15) | collective-permute-done | bytes 98336 | tf_op jit(solution)/shard_map/ppermute | solution.py:288
  91.3 3.6 %collective-permute-start.20 = (bf16[4,2,128,128]{3,2,1,0:T(8,128)(2,1)}, bf16[4,2,128,128]{3,2,1,0:T(8,128)(2,1)S(1)}, u32[]{:S(2)}, u32[]{:S(2)}) collective-permute-start(bf16[4,2,128,128]{3,2,1,0:T(8,128)(2,1)} %copy-done.7), channel_id=1, source_target_pairs={{0,16},{16,32},{32,48},{48,0},{64,80},{80,96},{96,112},{112,64},{1... | collective-permute-start | bytes 786440 | tf_op jit(solution)/shard_map/ppermute | solution.py:288
  94.8 2.7 %collective-permute-start.21 = (bf16[4,2,128,128]{3,2,1,0:T(8,128)(2,1)S(1)}, bf16[4,2,128,128]{3,2,1,0:T(8,128)(2,1)S(1)}, u32[]{:S(2)}, u32[]{:S(2)}) collective-permute-start(bf16[4,2,128,128]{3,2,1,0:T(8,128)(2,1)S(1)} %copy-done.6), channel_id=1, source_target_pairs={{0,32},{16,48},{32,0},{48,16},{64,96},{80,112},{96,64},{112,80},{1... | collective-permute-start | bytes 786440 | tf_op jit(solution)/shard_map/ppermute | solution.py:288
  97.5 0.1 collective-permute-start.19
  97.6 20.6 %while.12 = (s32[]{:T(128)}, f32[2,192,128]{2,1,0:T(8,128)S(1)}, s32[]{:T(128)}, s32[]{:T(128)}, u32[]{:T(128)}, /*index=5*/s32[]{:T(128)}, s32[]{:T(128)}) while((s32[]{:T(128)}, f32[2,192,128]{2,1,0:T(8,128)S(1)}, s32[]{:T(128)}, s32[]{:T(128)}, u32[]{:T(128)}, /*index=5*/s32[]{:T(128)}, s32[]{:T(128)}) %tuple.53), condition=%wide.region_1.2_spmd, body=%wide.region_0.1_spmd.sunk | while | flops 540688 | bytes 2949538 | solution.py:370
  97.7 0.1 collective-permute-start
  97.8 1.3 collective-permute-done
  99.1 0.1 collective-permute-start.1
  99.2 2.9 %collective-permute-done.1 = bf16[192,128]{1,0:T(8,128)(2,1)S(1)} collective-permute-done((bf16[192,128]{1,0:T(8,128)(2,1)S(1)}, bf16[192,128]{1,0:T(8,128)(2,1)S(1)}, u32[]{:S(2)}, u32[]{:S(2)}) %collective-permute-start.1) | collective-permute-done | bytes 49184 | tf_op jit(solution)/shard_map/while/body/ppermute | solution.py:296
  102.2 2.8 %collective-permute-start.2 = (bf16[192,128]{1,0:T(8,128)(2,1)S(1)}, bf16[192,128]{1,0:T(8,128)(2,1)S(1)}, u32[]{:S(2)}, u32[]{:S(2)}) collective-permute-start(bf16[192,128]{1,0:T(8,128)(2,1)S(1)} %add_convert_fusion.6), channel_id=1, source_target_pairs={{0,4},{1,5},{2,6},{3,7},{4,0},{5,1},{6,2},{7,3},{8,12},{9,13},{10,... | collective-permute-start | bytes 147464 | tf_op jit(solution)/shard_map/while/body/ppermute | solution.py:296
  105.0 1.7 %collective-permute-done.2 = bf16[192,128]{1,0:T(8,128)(2,1)S(1)} collective-permute-done((bf16[192,128]{1,0:T(8,128)(2,1)S(1)}, bf16[192,128]{1,0:T(8,128)(2,1)S(1)}, u32[]{:S(2)}, u32[]{:S(2)}) %collective-permute-start.2) | collective-permute-done | bytes 49184 | tf_op jit(solution)/shard_map/while/body/ppermute | solution.py:296
  106.7 0.1 collective-permute-start.3
  106.8 6.8 %collective-permute-done.3 = bf16[192,128]{1,0:T(8,128)(2,1)S(1)} collective-permute-done((bf16[192,128]{1,0:T(8,128)(2,1)S(1)}, bf16[192,128]{1,0:T(8,128)(2,1)S(1)}, u32[]{:S(2)}, u32[]{:S(2)}) %collective-permute-start.3) | collective-permute-done | bytes 49184 | tf_op jit(solution)/shard_map/while/body/ppermute | solution.py:300
  113.7 3.7 %collective-permute-start.4 = (bf16[192,128]{1,0:T(8,128)(2,1)S(1)}, bf16[192,128]{1,0:T(8,128)(2,1)S(1)}, u32[]{:S(2)}, u32[]{:S(2)}) collective-permute-start(bf16[192,128]{1,0:T(8,128)(2,1)S(1)} %add_convert_fusion.8), channel_id=1, source_target_pairs={{0,1},{1,0},{2,3},{3,2},{4,5},{5,4},{6,7},{7,6},{8,9},{9,8},{10,11... | collective-permute-start | bytes 147464 | tf_op jit(solution)/shard_map/while/body/ppermute | solution.py:292
  117.4 0.9 collective-permute-done.4
  118.3 0.7 settle.1
  119.0 0.5 collective-permute-start.23
  119.6 2.6 %collective-permute-start.24 = (bf16[352,128]{1,0:T(8,128)(2,1)S(1)}, bf16[352,128]{1,0:T(8,128)(2,1)S(1)}, u32[]{:S(2)}, u32[]{:S(2)}) collective-permute-start(bf16[352,128]{1,0:T(8,128)(2,1)S(1)} %get-tuple-element.132), channel_id=1, source_target_pairs={{0,128},{16,144},{32,160},{48,176},{64,192},{80,208},{96,224},{112... | collective-permute-start | bytes 270344 | tf_op jit(solution)/shard_map/ppermute | solution.py:283
  122.1 2.0 %collective-permute-start.25 = (bf16[352,128]{1,0:T(8,128)(2,1)S(1)}, bf16[352,128]{1,0:T(8,128)(2,1)S(1)}, u32[]{:S(2)}, u32[]{:S(2)}) collective-permute-start(bf16[352,128]{1,0:T(8,128)(2,1)S(1)} %get-tuple-element.133), channel_id=1, source_target_pairs={{0,192},{16,208},{32,224},{48,240},{64,0},{80,16},{96,32},{112,48}... | collective-permute-start | bytes 270344 | tf_op jit(solution)/shard_map/ppermute | solution.py:283
  124.1 1.9 %lay_rows.1 = (bf16[128,2560]{1,0:T(8,128)(2,1)}, bf16[128,2560]{1,0:T(8,128)(2,1)}) custom-call(s32[3]{0:T(128)S(1)} %pad_add_fusion.info, bf16[1280,128]{1,0:T(8,128)(2,1)S(1)} %get-tuple-element.100.d0, bf16[1280,128]{1,0:T(8,128)(2,1)S(1)} %collective-permute-done.17.d1, bf16[1280,128]{1,0:T(8,128)(2,1)S(1)} %collective-permute-done.19.d2, ...), custom_call_target="tpu_custom_call" | custom-call | tf_op jit(solution)/shard_map/lay_rows/pallas_call | solution.py:248
  126.0 0.7 collective-permute-done.24.p2
  126.8 1.1 copy-done
  127.9 1.4 %place.1 = (f32[128,512]{1,0:T(8,128)}, f32[128,512]{1,0:T(8,128)}, f32[48,512]{1,0:T(8,128)}, f32[48,512]{1,0:T(8,128)}) custom-call(s32[3]{0:T(128)S(1)} %pad_add_fusion.info, bf16[128,2560]{1,0:T(8,128)(2,1)S(1)} %copy-done, bf16[352,128]{1,0:T(8,128)(2,1)S(1)} %get-tuple-element.130.p0, bf16[352,128]{1,0:T(8,128)(2,1)S(1)} %collective-permute-done.23.p1, ...), custom_call_target="tpu_custom_call" | custom-call | tf_op jit(solution)/shard_map/place/pallas_call | solution.py:271
  (49 shorter events, 0.6 us)
Async XLA Ops:
  0.7 9.7 %copy-start.8 = (bf16[1,128,2560]{2,1,0:T(8,128)(2,1)S(1)}, bf16[1,128,2560]{2,1,0:T(8,128)(2,1)}, u32[]{:S(2)}) copy-start(bf16[1,128,2560]{2,1,0:T(8,128)(2,1)} %param.9) | copy-start | bytes 1966084
  0.7 9.7 %copy-start.9 = (bf16[1,128,2560]{2,1,0:T(8,128)(2,1)S(1)}, bf16[1,128,2560]{2,1,0:T(8,128)(2,1)}, u32[]{:S(2)}) copy-start(bf16[1,128,2560]{2,1,0:T(8,128)(2,1)} %param.14) | copy-start | bytes 1966084
  2.0 5.9 %collective-permute-start.5 = (bf16[2,176,128]{2,1,0:T(8,128)(2,1)S(1)}, bf16[2,176,128]{2,1,0:T(8,128)(2,1)S(1)}, u32[]{:S(2)}, u32[]{:S(2)}) collective-permute-start(bf16[2,176,128]{2,1,0:T(8,128)(2,1)S(1)} %get-tuple-element.156), channel_id=1, source_target_pairs={{0,64},{16,80},{32,96},{48,112},{64,128},{80,144},{96,160},{112,17... | collective-permute-start | bytes 270344 | tf_op jit(solution)/shard_map/ppermute | solution.py:283
  4.2 6.3 %collective-permute-start.6 = (bf16[2,176,128]{2,1,0:T(8,128)(2,1)S(1)}, bf16[2,176,128]{2,1,0:T(8,128)(2,1)S(1)}, u32[]{:S(2)}, u32[]{:S(2)}) collective-permute-start(bf16[2,176,128]{2,1,0:T(8,128)(2,1)S(1)} %get-tuple-element.157), channel_id=1, source_target_pairs={{0,128},{16,144},{32,160},{48,176},{64,192},{80,208},{96,224},{112... | collective-permute-start | bytes 270344 | tf_op jit(solution)/shard_map/ppermute | solution.py:283
  6.8 3.7 %collective-permute-start.7 = (bf16[2,176,128]{2,1,0:T(8,128)(2,1)S(1)}, bf16[2,176,128]{2,1,0:T(8,128)(2,1)S(1)}, u32[]{:S(2)}, u32[]{:S(2)}) collective-permute-start(bf16[2,176,128]{2,1,0:T(8,128)(2,1)S(1)} %get-tuple-element.154), channel_id=1, source_target_pairs={{0,192},{16,208},{32,224},{48,240},{64,0},{80,16},{96,32},{112,48}... | collective-permute-start | bytes 270344 | tf_op jit(solution)/shard_map/ppermute | solution.py:283
  11.4 8.0 %collective-permute-start.10 = (bf16[2,128,640]{2,1,0:T(8,128)(2,1)S(1)}, bf16[2,128,640]{2,1,0:T(8,128)(2,1)S(1)}, u32[]{:S(2)}, u32[]{:S(2)}) collective-permute-start(bf16[2,128,640]{2,1,0:T(8,128)(2,1)S(1)} %get-tuple-element.146), channel_id=1, source_target_pairs={{0,192},{16,208},{32,224},{48,240},{64,0},{80,16},{96,32},{112,48}... | collective-permute-start | bytes 983048 | tf_op jit(solution)/shard_map/ppermute | solution.py:283
  13.5 7.4 %copy-start.10 = (s32[16]{0:T(128)S(1)}, s32[16]{0:T(128)}, u32[]{:S(2)}) copy-start(s32[16]{0:T(128)} %param.15) | copy-start | bytes 196
  13.6 18.8 %collective-permute-start.11 = (bf16[4,2,176,128]{3,2,1,0:T(8,128)(2,1)S(1)}, bf16[4,2,176,128]{3,2,1,0:T(8,128)(2,1)S(1)}, u32[]{:S(2)}, u32[]{:S(2)}) collective-permute-start(bf16[4,2,176,128]{3,2,1,0:T(8,128)(2,1)S(1)} %pad_maximum_fusion.2.kv0), channel_id=1, source_target_pairs={{0,16},{16,32},{32,48},{48,0},{64,80},{80,96},{96,112},{112,64},{1... | collective-permute-start | bytes 1081352 | tf_op jit(solution)/shard_map/ppermute | solution.py:288
  15.6 27.1 %collective-permute-start.12 = (bf16[4,2,176,128]{3,2,1,0:T(8,128)(2,1)S(1)}, bf16[4,2,176,128]{3,2,1,0:T(8,128)(2,1)S(1)}, u32[]{:S(2)}, u32[]{:S(2)}) collective-permute-start(bf16[4,2,176,128]{3,2,1,0:T(8,128)(2,1)S(1)} %pad_maximum_fusion.2.kv0), channel_id=1, source_target_pairs={{0,32},{16,48},{32,0},{48,16},{64,96},{80,112},{96,64},{112,80},{1... | collective-permute-start | bytes 1081352 | tf_op jit(solution)/shard_map/ppermute | solution.py:288
  18.6 24.1 %collective-permute-start.13 = (bf16[4,2,176,128]{3,2,1,0:T(8,128)(2,1)S(1)}, bf16[4,2,176,128]{3,2,1,0:T(8,128)(2,1)S(1)}, u32[]{:S(2)}, u32[]{:S(2)}) collective-permute-start(bf16[4,2,176,128]{3,2,1,0:T(8,128)(2,1)S(1)} %pad_maximum_fusion.2.kv0), channel_id=1, source_target_pairs={{0,48},{16,0},{32,16},{48,32},{64,112},{80,64},{96,80},{112,96},{1... | collective-permute-start | bytes 1081352 | tf_op jit(solution)/shard_map/ppermute | solution.py:288
  19.4 10.1 %collective-permute-start.8 = (bf16[2,128,640]{2,1,0:T(8,128)(2,1)}, bf16[2,128,640]{2,1,0:T(8,128)(2,1)S(1)}, u32[]{:S(2)}, u32[]{:S(2)}) collective-permute-start(bf16[2,128,640]{2,1,0:T(8,128)(2,1)} %get-tuple-element.148), channel_id=1, source_target_pairs={{0,64},{16,80},{32,96},{48,112},{64,128},{80,144},{96,160},{112,17... | collective-permute-start | bytes 983048 | tf_op jit(solution)/shard_map/ppermute | solution.py:283
  19.4 13.0 %collective-permute-start.9 = (bf16[2,128,640]{2,1,0:T(8,128)(2,1)}, bf16[2,128,640]{2,1,0:T(8,128)(2,1)S(1)}, u32[]{:S(2)}, u32[]{:S(2)}) collective-permute-start(bf16[2,128,640]{2,1,0:T(8,128)(2,1)} %get-tuple-element.149), channel_id=1, source_target_pairs={{0,128},{16,144},{32,160},{48,176},{64,192},{80,208},{96,224},{112... | collective-permute-start | bytes 983048 | tf_op jit(solution)/shard_map/ppermute | solution.py:283
  69.2 0.7 copy-start.1
  69.9 0.7 copy-start.3
  70.6 0.7 copy-start.5
  71.3 0.7 copy-start.7
  72.0 22.8 %copy-start.6 = (bf16[4,2,128,128]{3,2,1,0:T(8,128)(2,1)S(1)}, bf16[4,2,128,128]{3,2,1,0:T(8,128)(2,1)}, u32[]{:S(2)}) copy-start(bf16[4,2,128,128]{3,2,1,0:T(8,128)(2,1)} %copy-done.5) | copy-start | bytes 786436
  72.0 25.5 %copy-start.4 = (bf16[4,2,128,128]{3,2,1,0:T(8,128)(2,1)S(1)}, bf16[4,2,128,128]{3,2,1,0:T(8,128)(2,1)}, u32[]{:S(2)}) copy-start(bf16[4,2,128,128]{3,2,1,0:T(8,128)(2,1)} %copy-done.3) | copy-start | bytes 786436
  72.0 25.5 %copy-start.2 = (bf16[1280,128]{1,0:T(8,128)(2,1)S(1)}, bf16[1280,128]{1,0:T(8,128)(2,1)}, u32[]{:S(2)}) copy-start(bf16[1280,128]{1,0:T(8,128)(2,1)} %copy-done.1) | copy-start | bytes 983044
  72.0 19.2 %collective-permute-start.17 = (bf16[1280,128]{1,0:T(8,128)(2,1)}, bf16[1280,128]{1,0:T(8,128)(2,1)S(1)}, u32[]{:S(2)}, u32[]{:S(2)}) collective-permute-start(bf16[1280,128]{1,0:T(8,128)(2,1)} %get-tuple-element.105), channel_id=1, source_target_pairs={{0,64},{16,80},{32,96},{48,112},{64,128},{80,144},{96,160},{112,17... | collective-permute-start | bytes 983048 | tf_op jit(solution)/shard_map/ppermute | solution.py:283
  72.0 19.2 %collective-permute-start.18 = (bf16[1280,128]{1,0:T(8,128)(2,1)}, bf16[1280,128]{1,0:T(8,128)(2,1)S(1)}, u32[]{:S(2)}, u32[]{:S(2)}) collective-permute-start(bf16[1280,128]{1,0:T(8,128)(2,1)} %get-tuple-element.106), channel_id=1, source_target_pairs={{0,192},{16,208},{32,224},{48,240},{64,0},{80,16},{96,32},{112,48}... | collective-permute-start | bytes 983048 | tf_op jit(solution)/shard_map/ppermute | solution.py:283
  74.7 11.0 %collective-permute-start.14 = (bf16[4,2,48,128]{3,2,1,0:T(8,128)(2,1)}, bf16[4,2,48,128]{3,2,1,0:T(8,128)(2,1)S(1)}, u32[]{:S(2)}, u32[]{:S(2)}) collective-permute-start(bf16[4,2,48,128]{3,2,1,0:T(8,128)(2,1)} %get-tuple-element.102), channel_id=1, source_target_pairs={{0,16},{16,32},{32,48},{48,0},{64,80},{80,96},{96,112},{112,64},{1... | collective-permute-start | bytes 294920 | tf_op jit(solution)/shard_map/ppermute | solution.py:288
  82.7 8.5 %collective-permute-start.15 = (bf16[4,2,48,128]{3,2,1,0:T(8,128)(2,1)}, bf16[4,2,48,128]{3,2,1,0:T(8,128)(2,1)S(1)}, u32[]{:S(2)}, u32[]{:S(2)}) collective-permute-start(bf16[4,2,48,128]{3,2,1,0:T(8,128)(2,1)} %get-tuple-element.103), channel_id=1, source_target_pairs={{0,32},{16,48},{32,0},{48,16},{64,96},{80,112},{96,64},{112,80},{1... | collective-permute-start | bytes 294920 | tf_op jit(solution)/shard_map/ppermute | solution.py:288
  82.7 8.5 %collective-permute-start.16 = (bf16[4,2,48,128]{3,2,1,0:T(8,128)(2,1)S(1)}, bf16[4,2,48,128]{3,2,1,0:T(8,128)(2,1)S(1)}, u32[]{:S(2)}, u32[]{:S(2)}) collective-permute-start(bf16[4,2,48,128]{3,2,1,0:T(8,128)(2,1)S(1)} %get-tuple-element.104), channel_id=1, source_target_pairs={{0,48},{16,0},{32,16},{48,32},{64,112},{80,64},{96,80},{112,96},{1... | collective-permute-start | bytes 294920 | tf_op jit(solution)/shard_map/ppermute | solution.py:288
  91.3 27.1 %collective-permute-start.20 = (bf16[4,2,128,128]{3,2,1,0:T(8,128)(2,1)}, bf16[4,2,128,128]{3,2,1,0:T(8,128)(2,1)S(1)}, u32[]{:S(2)}, u32[]{:S(2)}) collective-permute-start(bf16[4,2,128,128]{3,2,1,0:T(8,128)(2,1)} %copy-done.7), channel_id=1, source_target_pairs={{0,16},{16,32},{32,48},{48,0},{64,80},{80,96},{96,112},{112,64},{1... | collective-permute-start | bytes 786440 | tf_op jit(solution)/shard_map/ppermute | solution.py:288
  94.8 23.5 %collective-permute-start.21 = (bf16[4,2,128,128]{3,2,1,0:T(8,128)(2,1)S(1)}, bf16[4,2,128,128]{3,2,1,0:T(8,128)(2,1)S(1)}, u32[]{:S(2)}, u32[]{:S(2)}) collective-permute-start(bf16[4,2,128,128]{3,2,1,0:T(8,128)(2,1)S(1)} %copy-done.6), channel_id=1, source_target_pairs={{0,32},{16,48},{32,0},{48,16},{64,96},{80,112},{96,64},{112,80},{1... | collective-permute-start | bytes 786440 | tf_op jit(solution)/shard_map/ppermute | solution.py:288
  97.5 20.8 %collective-permute-start.22 = (bf16[4,2,128,128]{3,2,1,0:T(8,128)(2,1)S(1)}, bf16[4,2,128,128]{3,2,1,0:T(8,128)(2,1)S(1)}, u32[]{:S(2)}, u32[]{:S(2)}) collective-permute-start(bf16[4,2,128,128]{3,2,1,0:T(8,128)(2,1)S(1)} %copy-done.4), channel_id=1, source_target_pairs={{0,48},{16,0},{32,16},{48,32},{64,112},{80,64},{96,80},{112,96},{1... | collective-permute-start | bytes 786440 | tf_op jit(solution)/shard_map/ppermute | solution.py:288
  97.5 21.5 %collective-permute-start.19 = (bf16[1280,128]{1,0:T(8,128)(2,1)S(1)}, bf16[1280,128]{1,0:T(8,128)(2,1)S(1)}, u32[]{:S(2)}, u32[]{:S(2)}) collective-permute-start(bf16[1280,128]{1,0:T(8,128)(2,1)S(1)} %copy-done.2), channel_id=1, source_target_pairs={{0,128},{16,144},{32,160},{48,176},{64,192},{80,208},{96,224},{112... | collective-permute-start | bytes 983048 | tf_op jit(solution)/shard_map/ppermute | solution.py:283
  97.7 1.4 %collective-permute-start = (f32[192,128]{1,0:T(8,128)S(1)}, f32[192,128]{1,0:T(8,128)S(1)}, u32[]{:S(2)}, u32[]{:S(2)}) collective-permute-start(f32[192,128]{1,0:T(8,128)S(1)} %select_bitcast_fusion.2), channel_id=1, source_target_pairs={{0,1},{1,0},{2,3},{3,2},{4,5},{5,4},{6,7},{7,6},{8,9},{9,8},{10,11... | collective-permute-start | bytes 294920 | tf_op jit(solution)/shard_map/while/body/ppermute | solution.py:292
  99.1 3.0 %collective-permute-start.1 = (bf16[192,128]{1,0:T(8,128)(2,1)S(1)}, bf16[192,128]{1,0:T(8,128)(2,1)S(1)}, u32[]{:S(2)}, u32[]{:S(2)}) collective-permute-start(bf16[192,128]{1,0:T(8,128)(2,1)S(1)} %fusion.14), channel_id=1, source_target_pairs={{0,2},{1,3},{2,0},{3,1},{4,6},{5,7},{6,4},{7,5},{8,10},{9,11},{10,... | collective-permute-start | bytes 147464 | tf_op jit(solution)/shard_map/while/body/ppermute | solution.py:296
  102.2 4.5 %collective-permute-start.2 = (bf16[192,128]{1,0:T(8,128)(2,1)S(1)}, bf16[192,128]{1,0:T(8,128)(2,1)S(1)}, u32[]{:S(2)}, u32[]{:S(2)}) collective-permute-start(bf16[192,128]{1,0:T(8,128)(2,1)S(1)} %add_convert_fusion.6), channel_id=1, source_target_pairs={{0,4},{1,5},{2,6},{3,7},{4,0},{5,1},{6,2},{7,3},{8,12},{9,13},{10,... | collective-permute-start | bytes 147464 | tf_op jit(solution)/shard_map/while/body/ppermute | solution.py:296
  106.7 6.9 %collective-permute-start.3 = (bf16[192,128]{1,0:T(8,128)(2,1)S(1)}, bf16[192,128]{1,0:T(8,128)(2,1)S(1)}, u32[]{:S(2)}, u32[]{:S(2)}) collective-permute-start(bf16[192,128]{1,0:T(8,128)(2,1)S(1)} %add_convert_fusion.7), channel_id=1, source_target_pairs={{0,8},{1,9},{2,10},{3,11},{4,12},{5,13},{6,14},{7,15},{8,0},{9,1},... | collective-permute-start | bytes 147464 | tf_op jit(solution)/shard_map/while/body/ppermute | solution.py:300
  113.7 4.6 %collective-permute-start.4 = (bf16[192,128]{1,0:T(8,128)(2,1)S(1)}, bf16[192,128]{1,0:T(8,128)(2,1)S(1)}, u32[]{:S(2)}, u32[]{:S(2)}) collective-permute-start(bf16[192,128]{1,0:T(8,128)(2,1)S(1)} %add_convert_fusion.8), channel_id=1, source_target_pairs={{0,1},{1,0},{2,3},{3,2},{4,5},{5,4},{6,7},{7,6},{8,9},{9,8},{10,11... | collective-permute-start | bytes 147464 | tf_op jit(solution)/shard_map/while/body/ppermute | solution.py:292
  119.0 6.9 %collective-permute-start.23 = (bf16[352,128]{1,0:T(8,128)(2,1)S(1)}, bf16[352,128]{1,0:T(8,128)(2,1)S(1)}, u32[]{:S(2)}, u32[]{:S(2)}) collective-permute-start(bf16[352,128]{1,0:T(8,128)(2,1)S(1)} %get-tuple-element.131), channel_id=1, source_target_pairs={{0,64},{16,80},{32,96},{48,112},{64,128},{80,144},{96,160},{112,17... | collective-permute-start | bytes 270344 | tf_op jit(solution)/shard_map/ppermute | solution.py:283
  119.6 7.1 %collective-permute-start.24 = (bf16[352,128]{1,0:T(8,128)(2,1)S(1)}, bf16[352,128]{1,0:T(8,128)(2,1)S(1)}, u32[]{:S(2)}, u32[]{:S(2)}) collective-permute-start(bf16[352,128]{1,0:T(8,128)(2,1)S(1)} %get-tuple-element.132), channel_id=1, source_target_pairs={{0,128},{16,144},{32,160},{48,176},{64,192},{80,208},{96,224},{112... | collective-permute-start | bytes 270344 | tf_op jit(solution)/shard_map/ppermute | solution.py:283
  122.1 4.6 %collective-permute-start.25 = (bf16[352,128]{1,0:T(8,128)(2,1)S(1)}, bf16[352,128]{1,0:T(8,128)(2,1)S(1)}, u32[]{:S(2)}, u32[]{:S(2)}) collective-permute-start(bf16[352,128]{1,0:T(8,128)(2,1)S(1)} %get-tuple-element.133), channel_id=1, source_target_pairs={{0,192},{16,208},{32,224},{48,240},{64,0},{80,16},{96,32},{112,48}... | collective-permute-start | bytes 270344 | tf_op jit(solution)/shard_map/ppermute | solution.py:283
  126.8 1.1 copy-start
where the time goes:
time: 132 us; the launch traced here: 129 us
  starting transfers between devices  46.2 us (35%)
  waiting for transfers between devices  43.5 us (33%)
  Pallas kernels  30.5 us (23%)
  local copies, waits for them, and re-layouts  4.57 us (3%)
  other arithmetic  3.12 us (2%)
  between operations  1.48 us (1%)
    pallas_call x1, Pallas kernels, attend(): pl.pallas_call(attend_kernel, out_shape=[shaped((NY, 2, PROMPT_ROWS, HD),...  26.5 us
    ppermute x9, starting transfers between devices, z_shift(): return lax.ppermute(a, 'prefix', pairs)  22.2 us
    ppermute x12, starting transfers between devices, y_shift(): return lax.ppermute(a, 'prefix', pairs)  17.2 us
    ppermute x9, waiting for transfers between devices, z_shift(): return lax.ppermute(a, 'prefix', pairs)  16.2 us
    ppermute x12, waiting for transfers between devices, y_shift(): return lax.ppermute(a, 'prefix', pairs)  13.7 us
    ppermute x1, waiting for transfers between devices, far_swap(): return lax.ppermute(a, 'resp', [(i, i ^ 8) for i in range(16)])  6.83 us
    ppermute x2, waiting for transfers between devices, x_swap(): return lax.ppermute(a, 'resp', [(i, i ^ 2 * bit) for i in range(16)])  4.62 us
    unnamed x22, local copies, waits for them, and re-layouts  3.92 us
  transfers between devices with their start and end apart: 26, of which 13 were waited for; matrix products, arithmetic and copies ran while one was open for 1% of the time, Pallas kernels for 2%

commit v1 on v0

--- a/solution.py
+++ b/solution.py
@@ -85,7 +85,7 @@
     p0, p1, p2, p3,
     d0, d1, d2, d3,
     r0, r1, r2, r3,
-    qs, gs, ks, vs, kt, vt, kp, vp, kpt, vpt, dk, dv, dkp, dvp, os, dq, sent, sems,
+    qs, gs, ks, vs, kt, vt, kp, vp, kpt, vpt, dk, dv, dkp, dvp, os, dq, sent, moved, sems,
 ):
     y = info[0]
     z = info[1]
@@ -175,8 +175,10 @@
         copies.append(pltpu.make_async_copy(sent.at[s], r, sems.at[s]))
         copies[-1].start()
     for s, d in enumerate((d0, d1, d2, d3)):
-        d[:GROUP, :] = os[head_rows(y + s), :]
-        d[GROUP:, :] = dq[head_rows(y + s), :]
+        moved[s, :GROUP, :] = os[head_rows(y + s), :]
+        moved[s, GROUP:, :] = dq[head_rows(y + s), :]
+        copies.append(pltpu.make_async_copy(moved.at[s], d, sems.at[NZ + s]))
+        copies[-1].start()
     for s, p in enumerate((p0, p1, p2, p3)):
         zp = lax.rem(z + s, NZ)
         for b in range(NY):
@@ -194,7 +196,7 @@
         + [shaped((2 * GROUP, HD), BF16)] * NY
         + [shaped((NY, 2, BLOCK, HD), BF16)] * NZ,
         in_specs=[SMEM] + [VMEM] * 8,
-        out_specs=[VMEM] * 8 + [pl.BlockSpec(memory_space=pl.ANY)] * NZ,
+        out_specs=[VMEM] * NZ + [pl.BlockSpec(memory_space=pl.ANY)] * (NY + NZ),
         scratch_shapes=[pltpu.VMEM((ROWS, HD), BF16)] * 2
         + [pltpu.VMEM((RESP, HD), BF16)] * 2
         + [pltpu.VMEM((HD, RESP), BF16)] * 2
@@ -203,7 +205,11 @@
         + [pltpu.VMEM((RESP, HD), F32)] * 2
         + [pltpu.VMEM((PROMPT, HD), F32)] * 2
         + [pltpu.VMEM((ROWS, HD), BF16)] * 2
-        + [pltpu.VMEM((NZ, NY, 2, BLOCK, HD), BF16), pltpu.SemaphoreType.DMA((NZ,))],
+        + [
+            pltpu.VMEM((NZ, NY, 2, BLOCK, HD), BF16),
+            pltpu.VMEM((NY, 2 * GROUP, HD), BF16),
+            pltpu.SemaphoreType.DMA((NZ + NY,)),
+        ],
         compiler_params=pltpu.CompilerParams(vmem_limit_bytes=48 * 2**20),
         name="attend",
     )(info, *rows, *keyvals)
@@ -234,8 +240,9 @@
     )(info, *terms, prompt)
 
 
-def rows_kernel(info, d0, d1, d2, d3, att, dq):
+def rows_kernel(info, d0, d1, d2, d3, att, dq, done):
     y = info[0]
+    done[...] = jnp.zeros_like(done)
     for s, d in enumerate((d0, d1, d2, d3)):
         block = lax.rem(y - s + NY, NY)
         for j in range(HEADS):
@@ -247,9 +254,9 @@
 def lay_rows(info, pieces):
     return pl.pallas_call(
         rows_kernel,
-        out_shape=[shaped((BLOCK, NY * HEADS * HD), BF16)] * 2,
+        out_shape=[shaped((BLOCK, NY * HEADS * HD), BF16)] * 2 + [shaped((8, HD), F32)],
         in_specs=[SMEM] + [VMEM] * 4,
-        out_specs=[VMEM] * 2,
+        out_specs=[VMEM] * 3,
         compiler_params=pltpu.CompilerParams(vmem_limit_bytes=16 * 2**20),
         name="lay_rows",
     )(info, *pieces)
@@ -358,22 +365,22 @@
     results = attend(info, rows, keyvals)
     prompt_terms = by_z(results[:4])
     d0, d1, d2, d3 = results[4:8]
+    prompt_terms[1], d1, d3 = lax.optimization_barrier((prompt_terms[1], d1, d3))
     d1, d3 = y_shift(d1, 1), y_shift(d3, 3)
-    *prompt_terms, d1, d3, d2, t1, t2, t3 = lax.optimization_barrier(
-        (*prompt_terms, d1, d3, d2, *results[9:])
-    )
+    *prompt_terms, t1, t2, t3 = lax.optimization_barrier((*prompt_terms, *results[9:]))
     prompt = sum(t.astype(F32) for t in prompt_terms)
     prompt = prompt.transpose(1, 0, 2, 3).reshape(2, NY * PROMPT_ROWS, HD)
     once = jnp.minimum(lengths[0], 1)
     terms = by_z([results[8], t1, t2, t3])
+    prompt, d1, d3, d2 = lax.optimization_barrier((prompt, d1, d3, d2))
     d2 = y_shift(d2, 2)
     prompt = lax.fori_loop(0, once, lambda i, terms: over_responses(terms), prompt)
     prompt = prompt.reshape(2, NY, PROMPT_ROWS, HD).transpose(1, 0, 2, 3)
     pieces = settle(info, terms, prompt)
     d2, *pieces = lax.optimization_barrier((d2, *pieces))
-    attention_out, query_grad = lay_rows(info, (d0, d1, d2, d3))
+    attention_out, query_grad, done = lay_rows(info, (d0, d1, d2, d3))
     key_own, value_own, prompt_key_grad, prompt_value_grad = place(
-        info, query_grad, by_y(pieces)
+        info, done, by_y(pieces)
     )
     return (
         attention_out[None],

time: 132 us -> 130 us (0.985); the launches traced: 129 us -> 129 us
    ppermute x9, starting transfers between devices: 22.2 us -> 25.3 us  [z_shift(): return lax.ppermute(a, 'prefix', pairs)]
    ppermute x9, waiting for transfers between devices: 16.2 us -> 13.3 us  [z_shift(): return lax.ppermute(a, 'prefix', pairs)]
    ppermute x2, starting transfers between devices: 2.93 us -> 0.19 us  [x_swap(): return lax.ppermute(a, 'resp', [(i, i ^ 2 * bit) for i in range(16)])]
    ppermute x2, waiting for transfers between devices: 4.62 us -> 7.36 us  [x_swap(): return lax.ppermute(a, 'resp', [(i, i ^ 2 * bit) for i in range(16)])]
    unnamed x22 -> x20, local copies, waits for them, and re-layouts: 3.92 us -> 2.84 us
where the time goes in v1:
time: 130 us; the launch traced here: 129 us
  starting transfers between devices  46.1 us (35%)
  waiting for transfers between devices  43.9 us (34%)
  Pallas kernels  31.2 us (24%)
  local copies, waits for them, and re-layouts  3.5 us (3%)
  other arithmetic  3.12 us (2%)
  between operations  1.57 us (1%)
    pallas_call x1, Pallas kernels, attend(): pl.pallas_call(attend_kernel, out_shape=[shaped((NY, 2, PROMPT_ROWS, HD),...  27.2 us
    ppermute x9, starting transfers between devices, z_shift(): return lax.ppermute(a, 'prefix', pairs)  25.3 us
    ppermute x12, starting transfers between devices, y_shift(): return lax.ppermute(a, 'prefix', pairs)  16.6 us
    ppermute x12, waiting for transfers between devices, y_shift(): return lax.ppermute(a, 'prefix', pairs)  13.9 us
    ppermute x9, waiting for transfers between devices, z_shift(): return lax.ppermute(a, 'prefix', pairs)  13.3 us
    ppermute x2, waiting for transfers between devices, x_swap(): return lax.ppermute(a, 'resp', [(i, i ^ 2 * bit) for i in range(16)])  7.36 us
    ppermute x1, waiting for transfers between devices, far_swap(): return lax.ppermute(a, 'resp', [(i, i ^ 8) for i in range(16)])  7.25 us
    ppermute x2, starting transfers between devices, core_swap(): return lax.ppermute(a, 'resp', [(i, i ^ 1) for i in range(16)])  3.85 us
  transfers between devices with their start and end apart: 26, of which 13 were waited for; matrix products, arithmetic and copies ran while one was open for 1% of the time, Pallas kernels for 2%

profile of v1, /device:TPU:1, one launch (start us, length us, event | category | flops | bytes accessed | tf_op | source)
XLA Modules:
  0.0 129.4 jit_solution(16023740743306946175)
XLA Ops:
  0.8 1.1 maximum_bitcast_fusion
  2.0 2.2 %collective-permute-start.5 = (bf16[2,176,128]{2,1,0:T(8,128)(2,1)S(1)}, bf16[2,176,128]{2,1,0:T(8,128)(2,1)S(1)}, u32[]{:S(2)}, u32[]{:S(2)}) collective-permute-start(bf16[2,176,128]{2,1,0:T(8,128)(2,1)S(1)} %get-tuple-element.166), channel_id=1, source_target_pairs={{0,64},{16,80},{32,96},{48,112},{64,128},{80,144},{96,160},{112,17... | collective-permute-start | bytes 270344 | tf_op jit(solution)/shard_map/ppermute | solution.py:290
  4.2 2.6 %collective-permute-start.6 = (bf16[2,176,128]{2,1,0:T(8,128)(2,1)S(1)}, bf16[2,176,128]{2,1,0:T(8,128)(2,1)S(1)}, u32[]{:S(2)}, u32[]{:S(2)}) collective-permute-start(bf16[2,176,128]{2,1,0:T(8,128)(2,1)S(1)} %get-tuple-element.167), channel_id=1, source_target_pairs={{0,128},{16,144},{32,160},{48,176},{64,192},{80,208},{96,224},{112... | collective-permute-start | bytes 270344 | tf_op jit(solution)/shard_map/ppermute | solution.py:290
  6.8 1.1 collective-permute-start.7
  7.9 2.6 %collective-permute-done.6 = bf16[2,176,128]{2,1,0:T(8,128)(2,1)S(1)} collective-permute-done((bf16[2,176,128]{2,1,0:T(8,128)(2,1)S(1)}, bf16[2,176,128]{2,1,0:T(8,128)(2,1)S(1)}, u32[]{:S(2)}, u32[]{:S(2)}) %collective-permute-start.6) | collective-permute-done | bytes 90144 | tf_op jit(solution)/shard_map/ppermute | solution.py:290
  10.5 0.9 fusion.3
  11.4 2.0 %collective-permute-start.10 = (bf16[2,128,640]{2,1,0:T(8,128)(2,1)S(1)}, bf16[2,128,640]{2,1,0:T(8,128)(2,1)S(1)}, u32[]{:S(2)}, u32[]{:S(2)}) collective-permute-start(bf16[2,128,640]{2,1,0:T(8,128)(2,1)S(1)} %get-tuple-element.156), channel_id=1, source_target_pairs={{0,192},{16,208},{32,224},{48,240},{64,0},{80,16},{96,32},{112,48}... | collective-permute-start | bytes 983048 | tf_op jit(solution)/shard_map/ppermute | solution.py:290
  13.6 2.1 %collective-permute-start.11 = (bf16[4,2,176,128]{3,2,1,0:T(8,128)(2,1)S(1)}, bf16[4,2,176,128]{3,2,1,0:T(8,128)(2,1)S(1)}, u32[]{:S(2)}, u32[]{:S(2)}) collective-permute-start(bf16[4,2,176,128]{3,2,1,0:T(8,128)(2,1)S(1)} %pad_maximum_fusion.2.kv0), channel_id=1, source_target_pairs={{0,16},{16,32},{32,48},{48,0},{64,80},{80,96},{96,112},{112,64},{1... | collective-permute-start | bytes 1081352 | tf_op jit(solution)/shard_map/ppermute | solution.py:295
  15.6 3.0 %collective-permute-start.12 = (bf16[4,2,176,128]{3,2,1,0:T(8,128)(2,1)S(1)}, bf16[4,2,176,128]{3,2,1,0:T(8,128)(2,1)S(1)}, u32[]{:S(2)}, u32[]{:S(2)}) collective-permute-start(bf16[4,2,176,128]{3,2,1,0:T(8,128)(2,1)S(1)} %pad_maximum_fusion.2.kv0), channel_id=1, source_target_pairs={{0,32},{16,48},{32,0},{48,16},{64,96},{80,112},{96,64},{112,80},{1... | collective-permute-start | bytes 1081352 | tf_op jit(solution)/shard_map/ppermute | solution.py:295
  18.6 0.7 collective-permute-start.13
  19.4 1.5 %collective-permute-start.9 = (bf16[2,128,640]{2,1,0:T(8,128)(2,1)}, bf16[2,128,640]{2,1,0:T(8,128)(2,1)S(1)}, u32[]{:S(2)}, u32[]{:S(2)}) collective-permute-start(bf16[2,128,640]{2,1,0:T(8,128)(2,1)} %get-tuple-element.159), channel_id=1, source_target_pairs={{0,128},{16,144},{32,160},{48,176},{64,192},{80,208},{96,224},{112... | collective-permute-start | bytes 983048 | tf_op jit(solution)/shard_map/ppermute | solution.py:290
  20.8 0.6 fusion.11
  21.4 0.7 pad_add_fusion.info
  22.1 7.3 %collective-permute-done.8.x1 = bf16[2,128,640]{2,1,0:T(8,128)(2,1)S(1)} collective-permute-done((bf16[2,128,640]{2,1,0:T(8,128)(2,1)}, bf16[2,128,640]{2,1,0:T(8,128)(2,1)S(1)}, u32[]{:S(2)}, u32[]{:S(2)}) %collective-permute-start.8) | collective-permute-done | bytes 327712 | tf_op jit(solution)/shard_map/ppermute | solution.py:290
  29.5 2.9 %collective-permute-done.9.x2 = bf16[2,128,640]{2,1,0:T(8,128)(2,1)S(1)} collective-permute-done((bf16[2,128,640]{2,1,0:T(8,128)(2,1)}, bf16[2,128,640]{2,1,0:T(8,128)(2,1)S(1)}, u32[]{:S(2)}, u32[]{:S(2)}) %collective-permute-start.9) | collective-permute-done | bytes 327712 | tf_op jit(solution)/shard_map/ppermute | solution.py:290
  32.4 10.3 %collective-permute-done.12.kv2 = bf16[4,2,176,128]{3,2,1,0:T(8,128)(2,1)S(1)} collective-permute-done((bf16[4,2,176,128]{3,2,1,0:T(8,128)(2,1)S(1)}, bf16[4,2,176,128]{3,2,1,0:T(8,128)(2,1)S(1)}, u32[]{:S(2)}, u32[]{:S(2)}) %collective-permute-start.12) | collective-permute-done | bytes 360480 | tf_op jit(solution)/shard_map/ppermute | solution.py:295
  42.7 27.2 %attend.1 = (bf16[4,2,48,128]{3,2,1,0:T(8,128)(2,1)S(1)}, bf16[4,2,48,128]{3,2,1,0:T(8,128)(2,1)S(1)}, bf16[4,2,48,128]{3,2,1,0:T(8,128)(2,1)}, bf16[4,2,48,128]...) custom-call(s32[3]{0:T(128)S(1)} %pad_add_fusion.info, ...), custom_call_target="tpu_custom_call" | custom-call | tf_op jit(solution)/shard_map/attend/pallas_call | solution.py:193
  69.9 0.7 copy-done
  70.6 0.7 copy-done.2
  71.3 0.7 copy-done.4
  72.0 0.7 copy-done.6
  72.7 8.0 %collective-permute-start.14 = (bf16[4,2,48,128]{3,2,1,0:T(8,128)(2,1)S(1)}, bf16[4,2,48,128]{3,2,1,0:T(8,128)(2,1)S(1)}, u32[]{:S(2)}, u32[]{:S(2)}) collective-permute-start(bf16[4,2,48,128]{3,2,1,0:T(8,128)(2,1)S(1)} %get-tuple-element.107), channel_id=1, source_target_pairs={{0,16},{16,32},{32,48},{48,0},{64,80},{80,96},{96,112},{112,64},{1... | collective-permute-start | bytes 294920 | tf_op jit(solution)/shard_map/ppermute | solution.py:295
  80.7 2.2 %collective-permute-start.16 = (bf16[4,2,48,128]{3,2,1,0:T(8,128)(2,1)S(1)}, bf16[4,2,48,128]{3,2,1,0:T(8,128)(2,1)S(1)}, u32[]{:S(2)}, u32[]{:S(2)}) collective-permute-start(bf16[4,2,48,128]{3,2,1,0:T(8,128)(2,1)S(1)} %get-tuple-element.112), channel_id=1, source_target_pairs={{0,48},{16,0},{32,16},{48,32},{64,112},{80,64},{96,80},{112,96},{1... | collective-permute-start | bytes 294920 | tf_op jit(solution)/shard_map/ppermute | solution.py:295
  82.9 0.5 collective-permute-done.14
  83.4 2.7 %collective-permute-start.18 = (bf16[1280,128]{1,0:T(8,128)(2,1)}, bf16[1280,128]{1,0:T(8,128)(2,1)S(1)}, u32[]{:S(2)}, u32[]{:S(2)}) collective-permute-start(bf16[1280,128]{1,0:T(8,128)(2,1)} %get-tuple-element.121), channel_id=1, source_target_pairs={{0,192},{16,208},{32,224},{48,240},{64,0},{80,16},{96,32},{112,48}... | collective-permute-start | bytes 983048 | tf_op jit(solution)/shard_map/ppermute | solution.py:290
  86.7 2.4 %collective-permute-done.15 = bf16[4,2,48,128]{3,2,1,0:T(8,128)(2,1)S(1)} collective-permute-done((bf16[4,2,48,128]{3,2,1,0:T(8,128)(2,1)}, bf16[4,2,48,128]{3,2,1,0:T(8,128)(2,1)S(1)}, u32[]{:S(2)}, u32[]{:S(2)}) %collective-permute-start.15) | collective-permute-done | bytes 98336 | tf_op jit(solution)/shard_map/ppermute | solution.py:295
  89.2 5.3 %collective-permute-start.20 = (bf16[4,2,128,128]{3,2,1,0:T(8,128)(2,1)}, bf16[4,2,128,128]{3,2,1,0:T(8,128)(2,1)S(1)}, u32[]{:S(2)}, u32[]{:S(2)}) collective-permute-start(bf16[4,2,128,128]{3,2,1,0:T(8,128)(2,1)} %copy-done.6), channel_id=1, source_target_pairs={{0,16},{16,32},{32,48},{48,0},{64,80},{80,96},{96,112},{112,64},{1... | collective-permute-start | bytes 786440 | tf_op jit(solution)/shard_map/ppermute | solution.py:295
  94.6 1.7 %collective-permute-start.21 = (bf16[4,2,128,128]{3,2,1,0:T(8,128)(2,1)S(1)}, bf16[4,2,128,128]{3,2,1,0:T(8,128)(2,1)S(1)}, u32[]{:S(2)}, u32[]{:S(2)}) collective-permute-start(bf16[4,2,128,128]{3,2,1,0:T(8,128)(2,1)S(1)} %copy-done.5), channel_id=1, source_target_pairs={{0,32},{16,48},{32,0},{48,16},{64,96},{80,112},{96,64},{112,80},{1... | collective-permute-start | bytes 786440 | tf_op jit(solution)/shard_map/ppermute | solution.py:295
  96.3 2.3 %collective-permute-start.22 = (bf16[4,2,128,128]{3,2,1,0:T(8,128)(2,1)S(1)}, bf16[4,2,128,128]{3,2,1,0:T(8,128)(2,1)S(1)}, u32[]{:S(2)}, u32[]{:S(2)}) collective-permute-start(bf16[4,2,128,128]{3,2,1,0:T(8,128)(2,1)S(1)} %copy-done.3), channel_id=1, source_target_pairs={{0,48},{16,0},{32,16},{48,32},{64,112},{80,64},{96,80},{112,96},{1... | collective-permute-start | bytes 786440 | tf_op jit(solution)/shard_map/ppermute | solution.py:295
  98.6 0.1 collective-permute-start.19
  98.7 21.2 %while.12 = (s32[]{:T(128)}, f32[2,192,128]{2,1,0:T(8,128)S(1)}, s32[]{:T(128)}, s32[]{:T(128)}, u32[]{:T(128)}, /*index=5*/s32[]{:T(128)}, s32[]{:T(128)}) while((s32[]{:T(128)}, f32[2,192,128]{2,1,0:T(8,128)S(1)}, s32[]{:T(128)}, s32[]{:T(128)}, u32[]{:T(128)}, /*index=5*/s32[]{:T(128)}, s32[]{:T(128)}) %tuple.57), condition=%wide.region_1.2_spmd, body=%wide.region_0.1_spmd.sunk | while | flops 540688 | bytes 2949538 | solution.py:377
  98.7 0.1 collective-permute-start
  98.8 1.3 collective-permute-done
  100.1 0.1 collective-permute-start.1
  100.2 2.9 %collective-permute-done.1 = bf16[192,128]{1,0:T(8,128)(2,1)S(1)} collective-permute-done((bf16[192,128]{1,0:T(8,128)(2,1)S(1)}, bf16[192,128]{1,0:T(8,128)(2,1)S(1)}, u32[]{:S(2)}, u32[]{:S(2)}) %collective-permute-start.1) | collective-permute-done | bytes 49184 | tf_op jit(solution)/shard_map/while/body/ppermute | solution.py:303
  103.2 0.1 collective-permute-start.2
  103.3 4.4 %collective-permute-done.2 = bf16[192,128]{1,0:T(8,128)(2,1)S(1)} collective-permute-done((bf16[192,128]{1,0:T(8,128)(2,1)S(1)}, bf16[192,128]{1,0:T(8,128)(2,1)S(1)}, u32[]{:S(2)}, u32[]{:S(2)}) %collective-permute-start.2) | collective-permute-done | bytes 49184 | tf_op jit(solution)/shard_map/while/body/ppermute | solution.py:303
  107.7 0.2 collective-permute-start.3
  107.9 7.2 %collective-permute-done.3 = bf16[192,128]{1,0:T(8,128)(2,1)S(1)} collective-permute-done((bf16[192,128]{1,0:T(8,128)(2,1)S(1)}, bf16[192,128]{1,0:T(8,128)(2,1)S(1)}, u32[]{:S(2)}, u32[]{:S(2)}) %collective-permute-start.3) | collective-permute-done | bytes 49184 | tf_op jit(solution)/shard_map/while/body/ppermute | solution.py:307
  115.2 3.8 %collective-permute-start.4 = (bf16[192,128]{1,0:T(8,128)(2,1)S(1)}, bf16[192,128]{1,0:T(8,128)(2,1)S(1)}, u32[]{:S(2)}, u32[]{:S(2)}) collective-permute-start(bf16[192,128]{1,0:T(8,128)(2,1)S(1)} %add_convert_fusion.8), channel_id=1, source_target_pairs={{0,1},{1,0},{2,3},{3,2},{4,5},{5,4},{6,7},{7,6},{8,9},{9,8},{10,11... | collective-permute-start | bytes 147464 | tf_op jit(solution)/shard_map/while/body/ppermute | solution.py:299
  119.0 0.9 collective-permute-done.4
  120.0 0.7 settle.1
  120.8 2.4 %collective-permute-start.24 = (bf16[352,128]{1,0:T(8,128)(2,1)S(1)}, bf16[352,128]{1,0:T(8,128)(2,1)S(1)}, u32[]{:S(2)}, u32[]{:S(2)}) collective-permute-start(bf16[352,128]{1,0:T(8,128)(2,1)S(1)} %get-tuple-element.142), channel_id=1, source_target_pairs={{0,128},{16,144},{32,160},{48,176},{64,192},{80,208},{96,224},{112... | collective-permute-start | bytes 270344 | tf_op jit(solution)/shard_map/ppermute | solution.py:290
  123.2 2.0 %collective-permute-start.25 = (bf16[352,128]{1,0:T(8,128)(2,1)S(1)}, bf16[352,128]{1,0:T(8,128)(2,1)S(1)}, u32[]{:S(2)}, u32[]{:S(2)}) collective-permute-start(bf16[352,128]{1,0:T(8,128)(2,1)S(1)} %get-tuple-element.143), channel_id=1, source_target_pairs={{0,192},{16,208},{32,224},{48,240},{64,0},{80,16},{96,32},{112,48}... | collective-permute-start | bytes 270344 | tf_op jit(solution)/shard_map/ppermute | solution.py:290
  125.1 1.9 %lay_rows.1 = (bf16[128,2560]{1,0:T(8,128)(2,1)}, bf16[128,2560]{1,0:T(8,128)(2,1)}, f32[8,128]{1,0:T(8,128)S(1)}) custom-call(s32[3]{0:T(128)S(1)} %pad_add_fusion.info, bf16[1280,128]{1,0:T(8,128)(2,1)S(1)} %get-tuple-element.105.d0, bf16[1280,128]{1,0:T(8,128)(2,1)S(1)} %collective-permute-done.17.d1, bf16[1280,128]{1,0:T(8,128)(2,1)S(1)} %collective-permute-done.19.d2, ...), custom_call_target="tpu_custom_call" | custom-call | tf_op jit(solution)/shard_map/lay_rows/pallas_call | solution.py:255
  127.0 0.4 collective-permute-done.24.p2
  127.4 0.6 collective-permute-done.25.p3
  128.0 1.5 %place.1 = (f32[128,512]{1,0:T(8,128)}, f32[128,512]{1,0:T(8,128)}, f32[48,512]{1,0:T(8,128)}, f32[48,512]{1,0:T(8,128)}) custom-call(s32[3]{0:T(128)S(1)} %pad_add_fusion.info, f32[8,128]{1,0:T(8,128)S(1)} %get-tuple-element.139.done, bf16[352,128]{1,0:T(8,128)(2,1)S(1)} %get-tuple-element.140.p0, bf16[352,128]{1,0:T(8,128)(2,1)S(1)} %collective-permute-done.23.p1, ...), custom_call_target="tpu_custom_call" | custom-call | tf_op jit(solution)/shard_map/place/pallas_call | solution.py:278
  (47 shorter events, 0.6 us)
Async XLA Ops:
  0.7 9.7 %copy-start.7 = (bf16[1,128,2560]{2,1,0:T(8,128)(2,1)S(1)}, bf16[1,128,2560]{2,1,0:T(8,128)(2,1)}, u32[]{:S(2)}) copy-start(bf16[1,128,2560]{2,1,0:T(8,128)(2,1)} %param.9) | copy-start | bytes 1966084
  0.7 9.7 %copy-start.8 = (bf16[1,128,2560]{2,1,0:T(8,128)(2,1)S(1)}, bf16[1,128,2560]{2,1,0:T(8,128)(2,1)}, u32[]{:S(2)}) copy-start(bf16[1,128,2560]{2,1,0:T(8,128)(2,1)} %param.14) | copy-start | bytes 1966084
  2.0 5.9 %collective-permute-start.5 = (bf16[2,176,128]{2,1,0:T(8,128)(2,1)S(1)}, bf16[2,176,128]{2,1,0:T(8,128)(2,1)S(1)}, u32[]{:S(2)}, u32[]{:S(2)}) collective-permute-start(bf16[2,176,128]{2,1,0:T(8,128)(2,1)S(1)} %get-tuple-element.166), channel_id=1, source_target_pairs={{0,64},{16,80},{32,96},{48,112},{64,128},{80,144},{96,160},{112,17... | collective-permute-start | bytes 270344 | tf_op jit(solution)/shard_map/ppermute | solution.py:290
  4.2 6.3 %collective-permute-start.6 = (bf16[2,176,128]{2,1,0:T(8,128)(2,1)S(1)}, bf16[2,176,128]{2,1,0:T(8,128)(2,1)S(1)}, u32[]{:S(2)}, u32[]{:S(2)}) collective-permute-start(bf16[2,176,128]{2,1,0:T(8,128)(2,1)S(1)} %get-tuple-element.167), channel_id=1, source_target_pairs={{0,128},{16,144},{32,160},{48,176},{64,192},{80,208},{96,224},{112... | collective-permute-start | bytes 270344 | tf_op jit(solution)/shard_map/ppermute | solution.py:290
  6.8 3.7 %collective-permute-start.7 = (bf16[2,176,128]{2,1,0:T(8,128)(2,1)S(1)}, bf16[2,176,128]{2,1,0:T(8,128)(2,1)S(1)}, u32[]{:S(2)}, u32[]{:S(2)}) collective-permute-start(bf16[2,176,128]{2,1,0:T(8,128)(2,1)S(1)} %get-tuple-element.164), channel_id=1, source_target_pairs={{0,192},{16,208},{32,224},{48,240},{64,0},{80,16},{96,32},{112,48}... | collective-permute-start | bytes 270344 | tf_op jit(solution)/shard_map/ppermute | solution.py:290
  11.4 8.0 %collective-permute-start.10 = (bf16[2,128,640]{2,1,0:T(8,128)(2,1)S(1)}, bf16[2,128,640]{2,1,0:T(8,128)(2,1)S(1)}, u32[]{:S(2)}, u32[]{:S(2)}) collective-permute-start(bf16[2,128,640]{2,1,0:T(8,128)(2,1)S(1)} %get-tuple-element.156), channel_id=1, source_target_pairs={{0,192},{16,208},{32,224},{48,240},{64,0},{80,16},{96,32},{112,48}... | collective-permute-start | bytes 983048 | tf_op jit(solution)/shard_map/ppermute | solution.py:290
  13.5 7.4 %copy-start.9 = (s32[16]{0:T(128)S(1)}, s32[16]{0:T(128)}, u32[]{:S(2)}) copy-start(s32[16]{0:T(128)} %param.15) | copy-start | bytes 196
  13.6 18.8 %collective-permute-start.11 = (bf16[4,2,176,128]{3,2,1,0:T(8,128)(2,1)S(1)}, bf16[4,2,176,128]{3,2,1,0:T(8,128)(2,1)S(1)}, u32[]{:S(2)}, u32[]{:S(2)}) collective-permute-start(bf16[4,2,176,128]{3,2,1,0:T(8,128)(2,1)S(1)} %pad_maximum_fusion.2.kv0), channel_id=1, source_target_pairs={{0,16},{16,32},{32,48},{48,0},{64,80},{80,96},{96,112},{112,64},{1... | collective-permute-start | bytes 1081352 | tf_op jit(solution)/shard_map/ppermute | solution.py:295
  15.6 27.1 %collective-permute-start.12 = (bf16[4,2,176,128]{3,2,1,0:T(8,128)(2,1)S(1)}, bf16[4,2,176,128]{3,2,1,0:T(8,128)(2,1)S(1)}, u32[]{:S(2)}, u32[]{:S(2)}) collective-permute-start(bf16[4,2,176,128]{3,2,1,0:T(8,128)(2,1)S(1)} %pad_maximum_fusion.2.kv0), channel_id=1, source_target_pairs={{0,32},{16,48},{32,0},{48,16},{64,96},{80,112},{96,64},{112,80},{1... | collective-permute-start | bytes 1081352 | tf_op jit(solution)/shard_map/ppermute | solution.py:295
  18.6 24.1 %collective-permute-start.13 = (bf16[4,2,176,128]{3,2,1,0:T(8,128)(2,1)S(1)}, bf16[4,2,176,128]{3,2,1,0:T(8,128)(2,1)S(1)}, u32[]{:S(2)}, u32[]{:S(2)}) collective-permute-start(bf16[4,2,176,128]{3,2,1,0:T(8,128)(2,1)S(1)} %pad_maximum_fusion.2.kv0), channel_id=1, source_target_pairs={{0,48},{16,0},{32,16},{48,32},{64,112},{80,64},{96,80},{112,96},{1... | collective-permute-start | bytes 1081352 | tf_op jit(solution)/shard_map/ppermute | solution.py:295
  19.4 10.1 %collective-permute-start.8 = (bf16[2,128,640]{2,1,0:T(8,128)(2,1)}, bf16[2,128,640]{2,1,0:T(8,128)(2,1)S(1)}, u32[]{:S(2)}, u32[]{:S(2)}) collective-permute-start(bf16[2,128,640]{2,1,0:T(8,128)(2,1)} %get-tuple-element.158), channel_id=1, source_target_pairs={{0,64},{16,80},{32,96},{48,112},{64,128},{80,144},{96,160},{112,17... | collective-permute-start | bytes 983048 | tf_op jit(solution)/shard_map/ppermute | solution.py:290
  19.4 13.0 %collective-permute-start.9 = (bf16[2,128,640]{2,1,0:T(8,128)(2,1)}, bf16[2,128,640]{2,1,0:T(8,128)(2,1)S(1)}, u32[]{:S(2)}, u32[]{:S(2)}) collective-permute-start(bf16[2,128,640]{2,1,0:T(8,128)(2,1)} %get-tuple-element.159), channel_id=1, source_target_pairs={{0,128},{16,144},{32,160},{48,176},{64,192},{80,208},{96,224},{112... | collective-permute-start | bytes 983048 | tf_op jit(solution)/shard_map/ppermute | solution.py:290
  69.9 0.7 copy-start
  70.6 0.7 copy-start.2
  71.3 0.7 copy-start.4
  72.0 0.7 copy-start.6
  72.7 21.8 %copy-start.5 = (bf16[4,2,128,128]{3,2,1,0:T(8,128)(2,1)S(1)}, bf16[4,2,128,128]{3,2,1,0:T(8,128)(2,1)}, u32[]{:S(2)}) copy-start(bf16[4,2,128,128]{3,2,1,0:T(8,128)(2,1)} %copy-done.4) | copy-start | bytes 786436
  72.7 23.6 %copy-start.3 = (bf16[4,2,128,128]{3,2,1,0:T(8,128)(2,1)S(1)}, bf16[4,2,128,128]{3,2,1,0:T(8,128)(2,1)}, u32[]{:S(2)}) copy-start(bf16[4,2,128,128]{3,2,1,0:T(8,128)(2,1)} %copy-done.2) | copy-start | bytes 786436
  72.7 25.8 %copy-start.1 = (bf16[1280,128]{1,0:T(8,128)(2,1)S(1)}, bf16[1280,128]{1,0:T(8,128)(2,1)}, u32[]{:S(2)}) copy-start(bf16[1280,128]{1,0:T(8,128)(2,1)} %copy-done) | copy-start | bytes 983044
  72.7 10.7 %collective-permute-start.14 = (bf16[4,2,48,128]{3,2,1,0:T(8,128)(2,1)S(1)}, bf16[4,2,48,128]{3,2,1,0:T(8,128)(2,1)S(1)}, u32[]{:S(2)}, u32[]{:S(2)}) collective-permute-start(bf16[4,2,48,128]{3,2,1,0:T(8,128)(2,1)S(1)} %get-tuple-element.107), channel_id=1, source_target_pairs={{0,16},{16,32},{32,48},{48,0},{64,80},{80,96},{96,112},{112,64},{1... | collective-permute-start | bytes 294920 | tf_op jit(solution)/shard_map/ppermute | solution.py:295
  80.7 8.4 %collective-permute-start.15 = (bf16[4,2,48,128]{3,2,1,0:T(8,128)(2,1)}, bf16[4,2,48,128]{3,2,1,0:T(8,128)(2,1)S(1)}, u32[]{:S(2)}, u32[]{:S(2)}) collective-permute-start(bf16[4,2,48,128]{3,2,1,0:T(8,128)(2,1)} %get-tuple-element.111), channel_id=1, source_target_pairs={{0,32},{16,48},{32,0},{48,16},{64,96},{80,112},{96,64},{112,80},{1... | collective-permute-start | bytes 294920 | tf_op jit(solution)/shard_map/ppermute | solution.py:295
  80.7 8.4 %collective-permute-start.16 = (bf16[4,2,48,128]{3,2,1,0:T(8,128)(2,1)S(1)}, bf16[4,2,48,128]{3,2,1,0:T(8,128)(2,1)S(1)}, u32[]{:S(2)}, u32[]{:S(2)}) collective-permute-start(bf16[4,2,48,128]{3,2,1,0:T(8,128)(2,1)S(1)} %get-tuple-element.112), channel_id=1, source_target_pairs={{0,48},{16,0},{32,16},{48,32},{64,112},{80,64},{96,80},{112,96},{1... | collective-permute-start | bytes 294920 | tf_op jit(solution)/shard_map/ppermute | solution.py:295
  83.4 15.1 %collective-permute-start.17 = (bf16[1280,128]{1,0:T(8,128)(2,1)}, bf16[1280,128]{1,0:T(8,128)(2,1)S(1)}, u32[]{:S(2)}, u32[]{:S(2)}) collective-permute-start(bf16[1280,128]{1,0:T(8,128)(2,1)} %get-tuple-element.120), channel_id=1, source_target_pairs={{0,64},{16,80},{32,96},{48,112},{64,128},{80,144},{96,160},{112,17... | collective-permute-start | bytes 983048 | tf_op jit(solution)/shard_map/ppermute | solution.py:290
  83.4 15.1 %collective-permute-start.18 = (bf16[1280,128]{1,0:T(8,128)(2,1)}, bf16[1280,128]{1,0:T(8,128)(2,1)S(1)}, u32[]{:S(2)}, u32[]{:S(2)}) collective-permute-start(bf16[1280,128]{1,0:T(8,128)(2,1)} %get-tuple-element.121), channel_id=1, source_target_pairs={{0,192},{16,208},{32,224},{48,240},{64,0},{80,16},{96,32},{112,48}... | collective-permute-start | bytes 983048 | tf_op jit(solution)/shard_map/ppermute | solution.py:290
  89.2 30.7 %collective-permute-start.20 = (bf16[4,2,128,128]{3,2,1,0:T(8,128)(2,1)}, bf16[4,2,128,128]{3,2,1,0:T(8,128)(2,1)S(1)}, u32[]{:S(2)}, u32[]{:S(2)}) collective-permute-start(bf16[4,2,128,128]{3,2,1,0:T(8,128)(2,1)} %copy-done.6), channel_id=1, source_target_pairs={{0,16},{16,32},{32,48},{48,0},{64,80},{80,96},{96,112},{112,64},{1... | collective-permute-start | bytes 786440 | tf_op jit(solution)/shard_map/ppermute | solution.py:295
  94.6 25.4 %collective-permute-start.21 = (bf16[4,2,128,128]{3,2,1,0:T(8,128)(2,1)S(1)}, bf16[4,2,128,128]{3,2,1,0:T(8,128)(2,1)S(1)}, u32[]{:S(2)}, u32[]{:S(2)}) collective-permute-start(bf16[4,2,128,128]{3,2,1,0:T(8,128)(2,1)S(1)} %copy-done.5), channel_id=1, source_target_pairs={{0,32},{16,48},{32,0},{48,16},{64,96},{80,112},{96,64},{112,80},{1... | collective-permute-start | bytes 786440 | tf_op jit(solution)/shard_map/ppermute | solution.py:295
  96.3 23.7 %collective-permute-start.22 = (bf16[4,2,128,128]{3,2,1,0:T(8,128)(2,1)S(1)}, bf16[4,2,128,128]{3,2,1,0:T(8,128)(2,1)S(1)}, u32[]{:S(2)}, u32[]{:S(2)}) collective-permute-start(bf16[4,2,128,128]{3,2,1,0:T(8,128)(2,1)S(1)} %copy-done.3), channel_id=1, source_target_pairs={{0,48},{16,0},{32,16},{48,32},{64,112},{80,64},{96,80},{112,96},{1... | collective-permute-start | bytes 786440 | tf_op jit(solution)/shard_map/ppermute | solution.py:295
  98.6 22.1 %collective-permute-start.19 = (bf16[1280,128]{1,0:T(8,128)(2,1)S(1)}, bf16[1280,128]{1,0:T(8,128)(2,1)S(1)}, u32[]{:S(2)}, u32[]{:S(2)}) collective-permute-start(bf16[1280,128]{1,0:T(8,128)(2,1)S(1)} %copy-done.1), channel_id=1, source_target_pairs={{0,128},{16,144},{32,160},{48,176},{64,192},{80,208},{96,224},{112... | collective-permute-start | bytes 983048 | tf_op jit(solution)/shard_map/ppermute | solution.py:290
  98.7 1.4 %collective-permute-start = (f32[192,128]{1,0:T(8,128)S(1)}, f32[192,128]{1,0:T(8,128)S(1)}, u32[]{:S(2)}, u32[]{:S(2)}) collective-permute-start(f32[192,128]{1,0:T(8,128)S(1)} %select_bitcast_fusion.2), channel_id=1, source_target_pairs={{0,1},{1,0},{2,3},{3,2},{4,5},{5,4},{6,7},{7,6},{8,9},{9,8},{10,11... | collective-permute-start | bytes 294920 | tf_op jit(solution)/shard_map/while/body/ppermute | solution.py:299
  100.1 3.0 %collective-permute-start.1 = (bf16[192,128]{1,0:T(8,128)(2,1)S(1)}, bf16[192,128]{1,0:T(8,128)(2,1)S(1)}, u32[]{:S(2)}, u32[]{:S(2)}) collective-permute-start(bf16[192,128]{1,0:T(8,128)(2,1)S(1)} %fusion.14), channel_id=1, source_target_pairs={{0,2},{1,3},{2,0},{3,1},{4,6},{5,7},{6,4},{7,5},{8,10},{9,11},{10,... | collective-permute-start | bytes 147464 | tf_op jit(solution)/shard_map/while/body/ppermute | solution.py:303
  103.2 4.5 %collective-permute-start.2 = (bf16[192,128]{1,0:T(8,128)(2,1)S(1)}, bf16[192,128]{1,0:T(8,128)(2,1)S(1)}, u32[]{:S(2)}, u32[]{:S(2)}) collective-permute-start(bf16[192,128]{1,0:T(8,128)(2,1)S(1)} %add_convert_fusion.6), channel_id=1, source_target_pairs={{0,4},{1,5},{2,6},{3,7},{4,0},{5,1},{6,2},{7,3},{8,12},{9,13},{10,... | collective-permute-start | bytes 147464 | tf_op jit(solution)/shard_map/while/body/ppermute | solution.py:303
  107.7 7.5 %collective-permute-start.3 = (bf16[192,128]{1,0:T(8,128)(2,1)S(1)}, bf16[192,128]{1,0:T(8,128)(2,1)S(1)}, u32[]{:S(2)}, u32[]{:S(2)}) collective-permute-start(bf16[192,128]{1,0:T(8,128)(2,1)S(1)} %add_convert_fusion.7), channel_id=1, source_target_pairs={{0,8},{1,9},{2,10},{3,11},{4,12},{5,13},{6,14},{7,15},{8,0},{9,1},... | collective-permute-start | bytes 147464 | tf_op jit(solution)/shard_map/while/body/ppermute | solution.py:307
  115.2 4.6 %collective-permute-start.4 = (bf16[192,128]{1,0:T(8,128)(2,1)S(1)}, bf16[192,128]{1,0:T(8,128)(2,1)S(1)}, u32[]{:S(2)}, u32[]{:S(2)}) collective-permute-start(bf16[192,128]{1,0:T(8,128)(2,1)S(1)} %add_convert_fusion.8), channel_id=1, source_target_pairs={{0,1},{1,0},{2,3},{3,2},{4,5},{5,4},{6,7},{7,6},{8,9},{9,8},{10,11... | collective-permute-start | bytes 147464 | tf_op jit(solution)/shard_map/while/body/ppermute | solution.py:299
  120.7 6.3 %collective-permute-start.23 = (bf16[352,128]{1,0:T(8,128)(2,1)S(1)}, bf16[352,128]{1,0:T(8,128)(2,1)S(1)}, u32[]{:S(2)}, u32[]{:S(2)}) collective-permute-start(bf16[352,128]{1,0:T(8,128)(2,1)S(1)} %get-tuple-element.141), channel_id=1, source_target_pairs={{0,64},{16,80},{32,96},{48,112},{64,128},{80,144},{96,160},{112,17... | collective-permute-start | bytes 270344 | tf_op jit(solution)/shard_map/ppermute | solution.py:290
  120.8 6.7 %collective-permute-start.24 = (bf16[352,128]{1,0:T(8,128)(2,1)S(1)}, bf16[352,128]{1,0:T(8,128)(2,1)S(1)}, u32[]{:S(2)}, u32[]{:S(2)}) collective-permute-start(bf16[352,128]{1,0:T(8,128)(2,1)S(1)} %get-tuple-element.142), channel_id=1, source_target_pairs={{0,128},{16,144},{32,160},{48,176},{64,192},{80,208},{96,224},{112... | collective-permute-start | bytes 270344 | tf_op jit(solution)/shard_map/ppermute | solution.py:290
  123.2 4.8 %collective-permute-start.25 = (bf16[352,128]{1,0:T(8,128)(2,1)S(1)}, bf16[352,128]{1,0:T(8,128)(2,1)S(1)}, u32[]{:S(2)}, u32[]{:S(2)}) collective-permute-start(bf16[352,128]{1,0:T(8,128)(2,1)S(1)} %get-tuple-element.143), channel_id=1, source_target_pairs={{0,192},{16,208},{32,224},{48,240},{64,0},{80,16},{96,32},{112,48}... | collective-permute-start | bytes 270344 | tf_op jit(solution)/shard_map/ppermute | solution.py:290

commit v2 on v1

--- a/solution.py
+++ b/solution.py
@@ -193,10 +193,10 @@
     return pl.pallas_call(
         attend_kernel,
         out_shape=[shaped((NY, 2, PROMPT_ROWS, HD), BF16)] * NZ
-        + [shaped((2 * GROUP, HD), BF16)] * NY
-        + [shaped((NY, 2, BLOCK, HD), BF16)] * NZ,
+        + [pltpu.HBM((2 * GROUP, HD), BF16)] * NY
+        + [pltpu.HBM((NY, 2, BLOCK, HD), BF16)] * NZ,
         in_specs=[SMEM] + [VMEM] * 8,
-        out_specs=[VMEM] * NZ + [pl.BlockSpec(memory_space=pl.ANY)] * (NY + NZ),
+        out_specs=[VMEM] * NZ + [pl.BlockSpec(memory_space=pltpu.HBM)] * (NY + NZ),
         scratch_shapes=[pltpu.VMEM((ROWS, HD), BF16)] * 2
         + [pltpu.VMEM((RESP, HD), BF16)] * 2
         + [pltpu.VMEM((HD, RESP), BF16)] * 2
@@ -308,15 +308,10 @@
 
 
 def over_responses(terms):
-    core = lax.axis_index("resp") % 2
-    dk, dv = terms[0], terms[1]
-    half = jnp.where(core == 0, dk, dv) + core_swap(jnp.where(core == 0, dv, dk))
-    for swap in (lambda a: x_swap(a, 1), lambda a: x_swap(a, 2), far_swap):
-        low = half.astype(BF16)
-        half = low.astype(F32) + swap(low).astype(F32)
-    other = core_swap(half.astype(BF16)).astype(F32)
-    half = half.astype(BF16).astype(F32)
-    return jnp.stack([jnp.where(core == 0, half, other), jnp.where(core == 0, other, half)])
+    for swap in (core_swap, lambda a: x_swap(a, 1), lambda a: x_swap(a, 2), far_swap):
+        low = terms.astype(BF16)
+        terms = low.astype(F32) + swap(low).astype(F32)
+    return terms
 
 
 def by_y(pieces):

time: 130 us -> 128 us (0.985)
  the two profiles are of different devices: /device:TPU:1 before, /device:TPU:24 now
where the time goes in v2:
time: 128 us; the launch traced here: 126 us
  waiting for transfers between devices  52.6 us (41%)
  starting transfers between devices  37.9 us (30%)
  Pallas kernels  30.7 us (24%)
  other arithmetic  2.3 us (2%)
  between operations  1.61 us (1%)
    pallas_call x1, Pallas kernels, attend(): pl.pallas_call(attend_kernel, out_shape=[shaped((NY, 2, PROMPT_ROWS, HD),...  26.6 us
    ppermute x12, waiting for transfers between devices, y_shift(): return lax.ppermute(a, 'prefix', pairs)  21.5 us
    ppermute x9, waiting for transfers between devices, z_shift(): return lax.ppermute(a, 'prefix', pairs)  17.1 us
    ppermute x12, starting transfers between devices, y_shift(): return lax.ppermute(a, 'prefix', pairs)  15.4 us
    ppermute x9, starting transfers between devices, z_shift(): return lax.ppermute(a, 'prefix', pairs)  15.3 us
    ppermute x2, waiting for transfers between devices, x_swap(): return lax.ppermute(a, 'resp', [(i, i ^ 2 * bit) for i in range(16)])  9.15 us
    ppermute x1, starting transfers between devices, far_swap(): return lax.ppermute(a, 'resp', [(i, i ^ 8) for i in range(16)])  5.09 us
    ppermute x1, waiting for transfers between devices, far_swap(): return lax.ppermute(a, 'resp', [(i, i ^ 8) for i in range(16)])  3.56 us
  transfers between devices with their start and end apart: 25, of which 14 were waited for; matrix products, arithmetic and copies ran while one was open for 1% of the time, Pallas kernels for 2%

profile of v2, /device:TPU:24, one launch (start us, length us, event | category | flops | bytes accessed | tf_op | source)
XLA Modules:
  0.0 125.8 jit_solution(346174113052046372)
XLA Ops:
  0.8 1.1 maximum_bitcast_fusion
  1.9 0.1 fusion.4
  2.0 0.8 collective-permute-start.6
  2.8 2.5 %collective-permute-start.4 = (bf16[2,176,128]{2,1,0:T(8,128)(2,1)S(1)}, bf16[2,176,128]{2,1,0:T(8,128)(2,1)S(1)}, u32[]{:S(2)}, u32[]{:S(2)}) collective-permute-start(bf16[2,176,128]{2,1,0:T(8,128)(2,1)S(1)} %get-tuple-element.137), channel_id=1, source_target_pairs={{0,64},{16,80},{32,96},{48,112},{64,128},{80,144},{96,160},{112,17... | collective-permute-start | bytes 270344 | tf_op jit(solution)/shard_map/ppermute | solution.py:290
  5.3 0.2 collective-permute-start.5
  5.5 2.3 %collective-permute-done.6 = bf16[2,176,128]{2,1,0:T(8,128)(2,1)S(1)} collective-permute-done((bf16[2,176,128]{2,1,0:T(8,128)(2,1)S(1)}, bf16[2,176,128]{2,1,0:T(8,128)(2,1)S(1)}, u32[]{:S(2)}, u32[]{:S(2)}) %collective-permute-start.6) | collective-permute-done | bytes 90144 | tf_op jit(solution)/shard_map/ppermute | solution.py:290
  7.8 1.1 collective-permute-done.4
  8.8 2.5 %collective-permute-done.5 = bf16[2,176,128]{2,1,0:T(8,128)(2,1)S(1)} collective-permute-done((bf16[2,176,128]{2,1,0:T(8,128)(2,1)S(1)}, bf16[2,176,128]{2,1,0:T(8,128)(2,1)S(1)}, u32[]{:S(2)}, u32[]{:S(2)}) %collective-permute-start.5) | collective-permute-done | bytes 90144 | tf_op jit(solution)/shard_map/ppermute | solution.py:290
  11.3 0.1 fusion
  11.4 0.1 collective-permute-start.9
  11.6 0.0 copy-start.4
  11.7 4.7 %collective-permute-start.12 = (bf16[4,2,176,128]{3,2,1,0:T(8,128)(2,1)S(1)}, bf16[4,2,176,128]{3,2,1,0:T(8,128)(2,1)S(1)}, u32[]{:S(2)}, u32[]{:S(2)}) collective-permute-start(bf16[4,2,176,128]{3,2,1,0:T(8,128)(2,1)S(1)} %pad_maximum_fusion.1.kv0), channel_id=1, source_target_pairs={{0,48},{16,0},{32,16},{48,32},{64,112},{80,64},{96,80},{112,96},{1... | collective-permute-start | bytes 1081352 | tf_op jit(solution)/shard_map/ppermute | solution.py:295
  16.4 0.0 collective-permute-start.11
  16.4 0.7 collective-permute-start.10
  17.1 3.2 %collective-permute-start.7 = (bf16[2,128,640]{2,1,0:T(8,128)(2,1)S(1)}, bf16[2,128,640]{2,1,0:T(8,128)(2,1)S(1)}, u32[]{:S(2)}, u32[]{:S(2)}) collective-permute-start(bf16[2,128,640]{2,1,0:T(8,128)(2,1)S(1)} %get-tuple-element.129), channel_id=1, source_target_pairs={{0,64},{16,80},{32,96},{48,112},{64,128},{80,144},{96,160},{112,17... | collective-permute-start | bytes 983048 | tf_op jit(solution)/shard_map/ppermute | solution.py:290
  20.3 0.2 collective-permute-done.9.x3
  20.5 0.0 collective-permute-start.8
  20.5 0.6 fusion.8
  21.1 0.7 pad_add_fusion.info
  21.8 9.9 %collective-permute-done.7.x1 = bf16[2,128,640]{2,1,0:T(8,128)(2,1)S(1)} collective-permute-done((bf16[2,128,640]{2,1,0:T(8,128)(2,1)S(1)}, bf16[2,128,640]{2,1,0:T(8,128)(2,1)S(1)}, u32[]{:S(2)}, u32[]{:S(2)}) %collective-permute-start.7) | collective-permute-done | bytes 327712 | tf_op jit(solution)/shard_map/ppermute | solution.py:290
  31.7 13.2 %collective-permute-done.11.kv2 = bf16[4,2,176,128]{3,2,1,0:T(8,128)(2,1)S(1)} collective-permute-done((bf16[4,2,176,128]{3,2,1,0:T(8,128)(2,1)S(1)}, bf16[4,2,176,128]{3,2,1,0:T(8,128)(2,1)S(1)}, u32[]{:S(2)}, u32[]{:S(2)}) %collective-permute-start.11) | collective-permute-done | bytes 360480 | tf_op jit(solution)/shard_map/ppermute | solution.py:295
  44.9 26.6 %attend.1 = (bf16[4,2,48,128]{3,2,1,0:T(8,128)(2,1)S(1)}, bf16[4,2,48,128]{3,2,1,0:T(8,128)(2,1)S(1)}, bf16[4,2,48,128]{3,2,1,0:T(8,128)(2,1)S(1)}, bf16[4,2,48,...) custom-call(s32[3]{0:T(128)S(1)} %pad_add_fusion.info, ...), custom_call_target="tpu_custom_call" | custom-call | tf_op jit(solution)/shard_map/attend/pallas_call | solution.py:193
  71.6 1.4 %collective-permute-start.13 = (bf16[4,2,48,128]{3,2,1,0:T(8,128)(2,1)S(1)}, bf16[4,2,48,128]{3,2,1,0:T(8,128)(2,1)S(1)}, u32[]{:S(2)}, u32[]{:S(2)}) collective-permute-start(bf16[4,2,48,128]{3,2,1,0:T(8,128)(2,1)S(1)} %get-tuple-element.80), channel_id=1, source_target_pairs={{0,16},{16,32},{32,48},{48,0},{64,80},{80,96},{96,112},{112,64},{1... | collective-permute-start | bytes 294920 | tf_op jit(solution)/shard_map/ppermute | solution.py:295
  73.0 2.5 %collective-permute-start.15 = (bf16[4,2,48,128]{3,2,1,0:T(8,128)(2,1)S(1)}, bf16[4,2,48,128]{3,2,1,0:T(8,128)(2,1)S(1)}, u32[]{:S(2)}, u32[]{:S(2)}) collective-permute-start(bf16[4,2,48,128]{3,2,1,0:T(8,128)(2,1)S(1)} %get-tuple-element.85), channel_id=1, source_target_pairs={{0,48},{16,0},{32,16},{48,32},{64,112},{80,64},{96,80},{112,96},{1... | collective-permute-start | bytes 294920 | tf_op jit(solution)/shard_map/ppermute | solution.py:295
  75.5 3.9 %collective-permute-done.13 = bf16[4,2,48,128]{3,2,1,0:T(8,128)(2,1)S(1)} collective-permute-done((bf16[4,2,48,128]{3,2,1,0:T(8,128)(2,1)S(1)}, bf16[4,2,48,128]{3,2,1,0:T(8,128)(2,1)S(1)}, u32[]{:S(2)}, u32[]{:S(2)}) %collective-permute-start.13) | collective-permute-done | bytes 98336 | tf_op jit(solution)/shard_map/ppermute | solution.py:295
  79.4 2.9 %collective-permute-start.16 = (bf16[1280,128]{1,0:T(8,128)(2,1)}, bf16[1280,128]{1,0:T(8,128)(2,1)S(1)}, u32[]{:S(2)}, u32[]{:S(2)}) collective-permute-start(bf16[1280,128]{1,0:T(8,128)(2,1)} %get-tuple-element.93), channel_id=1, source_target_pairs={{0,64},{16,80},{32,96},{48,112},{64,128},{80,144},{96,160},{112,17... | collective-permute-start | bytes 983048 | tf_op jit(solution)/shard_map/ppermute | solution.py:290
  83.0 0.1 add_bitcast_fusion
  83.1 1.3 %collective-permute-start.19 = (bf16[4,2,128,128]{3,2,1,0:T(8,128)(2,1)}, bf16[4,2,128,128]{3,2,1,0:T(8,128)(2,1)S(1)}, u32[]{:S(2)}, u32[]{:S(2)}) collective-permute-start(bf16[4,2,128,128]{3,2,1,0:T(8,128)(2,1)} %get-tuple-element.99), channel_id=1, source_target_pairs={{0,16},{16,32},{32,48},{48,0},{64,80},{80,96},{96,112},{112,64},{1... | collective-permute-start | bytes 786440 | tf_op jit(solution)/shard_map/ppermute | solution.py:295
  84.4 1.9 %collective-permute-start.20 = (bf16[4,2,128,128]{3,2,1,0:T(8,128)(2,1)}, bf16[4,2,128,128]{3,2,1,0:T(8,128)(2,1)S(1)}, u32[]{:S(2)}, u32[]{:S(2)}) collective-permute-start(bf16[4,2,128,128]{3,2,1,0:T(8,128)(2,1)} %get-tuple-element.100), channel_id=1, source_target_pairs={{0,32},{16,48},{32,0},{48,16},{64,96},{80,112},{96,64},{112,80},{1... | collective-permute-start | bytes 786440 | tf_op jit(solution)/shard_map/ppermute | solution.py:295
  86.3 2.8 %collective-permute-start.21 = (bf16[4,2,128,128]{3,2,1,0:T(8,128)(2,1)S(1)}, bf16[4,2,128,128]{3,2,1,0:T(8,128)(2,1)S(1)}, u32[]{:S(2)}, u32[]{:S(2)}) collective-permute-start(bf16[4,2,128,128]{3,2,1,0:T(8,128)(2,1)S(1)} %copy-done.6), channel_id=1, source_target_pairs={{0,48},{16,0},{32,16},{48,32},{64,112},{80,64},{96,80},{112,96},{1... | collective-permute-start | bytes 786440 | tf_op jit(solution)/shard_map/ppermute | solution.py:295
  89.1 1.7 %collective-permute-done.17.d3 = bf16[1280,128]{1,0:T(8,128)(2,1)S(1)} collective-permute-done((bf16[1280,128]{1,0:T(8,128)(2,1)}, bf16[1280,128]{1,0:T(8,128)(2,1)S(1)}, u32[]{:S(2)}, u32[]{:S(2)}) %collective-permute-start.17) | collective-permute-done | bytes 327712 | tf_op jit(solution)/shard_map/ppermute | solution.py:290
  90.8 21.4 %while.10 = (s32[]{:T(128)}, f32[2,192,128]{2,1,0:T(8,128)S(1)}, s32[]{:T(128)}, s32[]{:T(128)}) while((s32[]{:T(128)}, f32[2,192,128]{2,1,0:T(8,128)S(1)}, s32[]{:T(128)}, s32[]{:T(128)}) %tuple.46), condition=%wide.region_1.2_spmd, body=%wide.region_0.1_spmd.sunk | while | flops 835586 | bytes 3244245 | solution.py:372
  90.9 0.1 collective-permute-start
  91.0 1.3 %collective-permute-done = bf16[2,192,128]{2,1,0:T(8,128)(2,1)S(1)} collective-permute-done((bf16[2,192,128]{2,1,0:T(8,128)(2,1)S(1)}, bf16[2,192,128]{2,1,0:T(8,128)(2,1)S(1)}, u32[]{:S(2)}, u32[]{:S(2)}) %collective-permute-start) | collective-permute-done | bytes 98336 | tf_op jit(solution)/shard_map/while/body/ppermute | solution.py:299
  92.3 0.1 collective-permute-start.1
  92.4 4.8 %collective-permute-done.1 = bf16[2,192,128]{2,1,0:T(8,128)(2,1)S(1)} collective-permute-done((bf16[2,192,128]{2,1,0:T(8,128)(2,1)S(1)}, bf16[2,192,128]{2,1,0:T(8,128)(2,1)S(1)}, u32[]{:S(2)}, u32[]{:S(2)}) %collective-permute-start.1) | collective-permute-done | bytes 98336 | tf_op jit(solution)/shard_map/while/body/ppermute | solution.py:303
  97.3 1.9 %collective-permute-start.2 = (bf16[2,192,128]{2,1,0:T(8,128)(2,1)S(1)}, bf16[2,192,128]{2,1,0:T(8,128)(2,1)S(1)}, u32[]{:S(2)}, u32[]{:S(2)}) collective-permute-start(bf16[2,192,128]{2,1,0:T(8,128)(2,1)S(1)} %add_convert_fusion.7), channel_id=1, source_target_pairs={{0,4},{1,5},{2,6},{3,7},{4,0},{5,1},{6,2},{7,3},{8,12},{9,13},{10,... | collective-permute-start | bytes 294920 | tf_op jit(solution)/shard_map/while/body/ppermute | solution.py:303
  99.2 4.3 %collective-permute-done.2 = bf16[2,192,128]{2,1,0:T(8,128)(2,1)S(1)} collective-permute-done((bf16[2,192,128]{2,1,0:T(8,128)(2,1)S(1)}, bf16[2,192,128]{2,1,0:T(8,128)(2,1)S(1)}, u32[]{:S(2)}, u32[]{:S(2)}) %collective-permute-start.2) | collective-permute-done | bytes 98336 | tf_op jit(solution)/shard_map/while/body/ppermute | solution.py:303
  103.5 5.1 %collective-permute-start.3 = (bf16[2,192,128]{2,1,0:T(8,128)(2,1)S(1)}, bf16[2,192,128]{2,1,0:T(8,128)(2,1)S(1)}, u32[]{:S(2)}, u32[]{:S(2)}) collective-permute-start(bf16[2,192,128]{2,1,0:T(8,128)(2,1)S(1)} %add_convert_fusion.8), channel_id=1, source_target_pairs={{0,8},{1,9},{2,10},{3,11},{4,12},{5,13},{6,14},{7,15},{8,0},{9,1},... | collective-permute-start | bytes 294920 | tf_op jit(solution)/shard_map/while/body/ppermute | solution.py:307
  108.6 3.6 %collective-permute-done.3 = bf16[2,192,128]{2,1,0:T(8,128)(2,1)S(1)} collective-permute-done((bf16[2,192,128]{2,1,0:T(8,128)(2,1)S(1)}, bf16[2,192,128]{2,1,0:T(8,128)(2,1)S(1)}, u32[]{:S(2)}, u32[]{:S(2)}) %collective-permute-start.3) | collective-permute-done | bytes 98336 | tf_op jit(solution)/shard_map/while/body/ppermute | solution.py:307
  112.2 0.0 copy-start
  112.3 0.7 settle.1
  113.0 1.8 %collective-permute-start.22 = (bf16[352,128]{1,0:T(8,128)(2,1)S(1)}, bf16[352,128]{1,0:T(8,128)(2,1)S(1)}, u32[]{:S(2)}, u32[]{:S(2)}) collective-permute-start(bf16[352,128]{1,0:T(8,128)(2,1)S(1)} %get-tuple-element.114), channel_id=1, source_target_pairs={{0,64},{16,80},{32,96},{48,112},{64,128},{80,144},{96,160},{112,17... | collective-permute-start | bytes 270344 | tf_op jit(solution)/shard_map/ppermute | solution.py:290
  114.7 3.9 %collective-permute-start.23 = (bf16[352,128]{1,0:T(8,128)(2,1)S(1)}, bf16[352,128]{1,0:T(8,128)(2,1)S(1)}, u32[]{:S(2)}, u32[]{:S(2)}) collective-permute-start(bf16[352,128]{1,0:T(8,128)(2,1)S(1)} %get-tuple-element.115), channel_id=1, source_target_pairs={{0,128},{16,144},{32,160},{48,176},{64,192},{80,208},{96,224},{112... | collective-permute-start | bytes 270344 | tf_op jit(solution)/shard_map/ppermute | solution.py:290
  118.6 1.9 %lay_rows.1 = (bf16[128,2560]{1,0:T(8,128)(2,1)}, bf16[128,2560]{1,0:T(8,128)(2,1)}, f32[8,128]{1,0:T(8,128)S(1)}) custom-call(s32[3]{0:T(128)S(1)} %pad_add_fusion.info, bf16[1280,128]{1,0:T(8,128)(2,1)S(1)} %copy-done, bf16[1280,128]{1,0:T(8,128)(2,1)S(1)} %collective-permute-done.16.d1, bf16[1280,128]{1,0:T(8,128)(2,1)S(1)} %collective-permute-done.18.d2, ...), custom_call_target="tpu_custom_call" | custom-call | tf_op jit(solution)/shard_map/lay_rows/pallas_call | solution.py:255
  120.5 0.6 collective-permute-done.23.p2
  121.1 3.2 %collective-permute-done.24.p3 = bf16[352,128]{1,0:T(8,128)(2,1)S(1)} collective-permute-done((bf16[352,128]{1,0:T(8,128)(2,1)S(1)}, bf16[352,128]{1,0:T(8,128)(2,1)S(1)}, u32[]{:S(2)}, u32[]{:S(2)}) %collective-permute-start.24) | collective-permute-done | bytes 90144 | tf_op jit(solution)/shard_map/ppermute | solution.py:290
  124.3 1.5 %place.1 = (f32[128,512]{1,0:T(8,128)}, f32[128,512]{1,0:T(8,128)}, f32[48,512]{1,0:T(8,128)}, f32[48,512]{1,0:T(8,128)}) custom-call(s32[3]{0:T(128)S(1)} %pad_add_fusion.info, f32[8,128]{1,0:T(8,128)S(1)} %get-tuple-element.112.done, bf16[352,128]{1,0:T(8,128)(2,1)S(1)} %get-tuple-element.113.p0, bf16[352,128]{1,0:T(8,128)(2,1)S(1)} %collective-permute-done.22.p1, ...), custom_call_target="tpu_custom_call" | custom-call | tf_op jit(solution)/shard_map/place/pallas_call | solution.py:278
  (37 shorter events, 0.3 us)
Async XLA Ops:
  0.7 10.6 %copy-start.2 = (bf16[1,128,2560]{2,1,0:T(8,128)(2,1)S(1)}, bf16[1,128,2560]{2,1,0:T(8,128)(2,1)}, u32[]{:S(2)}) copy-start(bf16[1,128,2560]{2,1,0:T(8,128)(2,1)} %param.9) | copy-start | bytes 1966084
  0.7 10.6 %copy-start.3 = (bf16[1,128,2560]{2,1,0:T(8,128)(2,1)S(1)}, bf16[1,128,2560]{2,1,0:T(8,128)(2,1)}, u32[]{:S(2)}) copy-start(bf16[1,128,2560]{2,1,0:T(8,128)(2,1)} %param.14) | copy-start | bytes 1966084
  2.0 5.8 %collective-permute-start.6 = (bf16[2,176,128]{2,1,0:T(8,128)(2,1)S(1)}, bf16[2,176,128]{2,1,0:T(8,128)(2,1)S(1)}, u32[]{:S(2)}, u32[]{:S(2)}) collective-permute-start(bf16[2,176,128]{2,1,0:T(8,128)(2,1)S(1)} %get-tuple-element.135), channel_id=1, source_target_pairs={{0,192},{16,208},{32,224},{48,240},{64,0},{80,16},{96,32},{112,48}... | collective-permute-start | bytes 270344 | tf_op jit(solution)/shard_map/ppermute | solution.py:290
  2.8 6.1 %collective-permute-start.4 = (bf16[2,176,128]{2,1,0:T(8,128)(2,1)S(1)}, bf16[2,176,128]{2,1,0:T(8,128)(2,1)S(1)}, u32[]{:S(2)}, u32[]{:S(2)}) collective-permute-start(bf16[2,176,128]{2,1,0:T(8,128)(2,1)S(1)} %get-tuple-element.137), channel_id=1, source_target_pairs={{0,64},{16,80},{32,96},{48,112},{64,128},{80,144},{96,160},{112,17... | collective-permute-start | bytes 270344 | tf_op jit(solution)/shard_map/ppermute | solution.py:290
  5.3 6.0 %collective-permute-start.5 = (bf16[2,176,128]{2,1,0:T(8,128)(2,1)S(1)}, bf16[2,176,128]{2,1,0:T(8,128)(2,1)S(1)}, u32[]{:S(2)}, u32[]{:S(2)}) collective-permute-start(bf16[2,176,128]{2,1,0:T(8,128)(2,1)S(1)} %get-tuple-element.138), channel_id=1, source_target_pairs={{0,128},{16,144},{32,160},{48,176},{64,192},{80,208},{96,224},{112... | collective-permute-start | bytes 270344 | tf_op jit(solution)/shard_map/ppermute | solution.py:290
  11.4 9.0 %collective-permute-start.9 = (bf16[2,128,640]{2,1,0:T(8,128)(2,1)S(1)}, bf16[2,128,640]{2,1,0:T(8,128)(2,1)S(1)}, u32[]{:S(2)}, u32[]{:S(2)}) collective-permute-start(bf16[2,128,640]{2,1,0:T(8,128)(2,1)S(1)} %get-tuple-element.127), channel_id=1, source_target_pairs={{0,192},{16,208},{32,224},{48,240},{64,0},{80,16},{96,32},{112,48}... | collective-permute-start | bytes 983048 | tf_op jit(solution)/shard_map/ppermute | solution.py:290
  11.6 8.9 %copy-start.4 = (s32[16]{0:T(128)S(1)}, s32[16]{0:T(128)}, u32[]{:S(2)}) copy-start(s32[16]{0:T(128)} %param.15) | copy-start | bytes 196
  11.7 20.0 %collective-permute-start.12 = (bf16[4,2,176,128]{3,2,1,0:T(8,128)(2,1)S(1)}, bf16[4,2,176,128]{3,2,1,0:T(8,128)(2,1)S(1)}, u32[]{:S(2)}, u32[]{:S(2)}) collective-permute-start(bf16[4,2,176,128]{3,2,1,0:T(8,128)(2,1)S(1)} %pad_maximum_fusion.1.kv0), channel_id=1, source_target_pairs={{0,48},{16,0},{32,16},{48,32},{64,112},{80,64},{96,80},{112,96},{1... | collective-permute-start | bytes 1081352 | tf_op jit(solution)/shard_map/ppermute | solution.py:295
  16.4 28.5 %collective-permute-start.11 = (bf16[4,2,176,128]{3,2,1,0:T(8,128)(2,1)S(1)}, bf16[4,2,176,128]{3,2,1,0:T(8,128)(2,1)S(1)}, u32[]{:S(2)}, u32[]{:S(2)}) collective-permute-start(bf16[4,2,176,128]{3,2,1,0:T(8,128)(2,1)S(1)} %pad_maximum_fusion.1.kv0), channel_id=1, source_target_pairs={{0,32},{16,48},{32,0},{48,16},{64,96},{80,112},{96,64},{112,80},{1... | collective-permute-start | bytes 1081352 | tf_op jit(solution)/shard_map/ppermute | solution.py:295
  16.4 28.5 %collective-permute-start.10 = (bf16[4,2,176,128]{3,2,1,0:T(8,128)(2,1)S(1)}, bf16[4,2,176,128]{3,2,1,0:T(8,128)(2,1)S(1)}, u32[]{:S(2)}, u32[]{:S(2)}) collective-permute-start(bf16[4,2,176,128]{3,2,1,0:T(8,128)(2,1)S(1)} %pad_maximum_fusion.1.kv0), channel_id=1, source_target_pairs={{0,16},{16,32},{32,48},{48,0},{64,80},{80,96},{96,112},{112,64},{1... | collective-permute-start | bytes 1081352 | tf_op jit(solution)/shard_map/ppermute | solution.py:295
  17.1 14.6 %collective-permute-start.7 = (bf16[2,128,640]{2,1,0:T(8,128)(2,1)S(1)}, bf16[2,128,640]{2,1,0:T(8,128)(2,1)S(1)}, u32[]{:S(2)}, u32[]{:S(2)}) collective-permute-start(bf16[2,128,640]{2,1,0:T(8,128)(2,1)S(1)} %get-tuple-element.129), channel_id=1, source_target_pairs={{0,64},{16,80},{32,96},{48,112},{64,128},{80,144},{96,160},{112,17... | collective-permute-start | bytes 983048 | tf_op jit(solution)/shard_map/ppermute | solution.py:290
  20.5 11.3 %collective-permute-start.8 = (bf16[2,128,640]{2,1,0:T(8,128)(2,1)S(1)}, bf16[2,128,640]{2,1,0:T(8,128)(2,1)S(1)}, u32[]{:S(2)}, u32[]{:S(2)}) collective-permute-start(bf16[2,128,640]{2,1,0:T(8,128)(2,1)S(1)} %get-tuple-element.130), channel_id=1, source_target_pairs={{0,128},{16,144},{32,160},{48,176},{64,192},{80,208},{96,224},{112... | collective-permute-start | bytes 983048 | tf_op jit(solution)/shard_map/ppermute | solution.py:290
  71.6 14.7 %copy-start.6 = (bf16[4,2,128,128]{3,2,1,0:T(8,128)(2,1)S(1)}, bf16[4,2,128,128]{3,2,1,0:T(8,128)(2,1)}, u32[]{:S(2)}) copy-start(bf16[4,2,128,128]{3,2,1,0:T(8,128)(2,1)} %get-tuple-element.101) | copy-start | bytes 786436
  71.6 19.2 %copy-start.5 = (bf16[1280,128]{1,0:T(8,128)(2,1)S(1)}, bf16[1280,128]{1,0:T(8,128)(2,1)}, u32[]{:S(2)}) copy-start(bf16[1280,128]{1,0:T(8,128)(2,1)} %get-tuple-element.97) | copy-start | bytes 983044
  71.6 7.8 %collective-permute-start.13 = (bf16[4,2,48,128]{3,2,1,0:T(8,128)(2,1)S(1)}, bf16[4,2,48,128]{3,2,1,0:T(8,128)(2,1)S(1)}, u32[]{:S(2)}, u32[]{:S(2)}) collective-permute-start(bf16[4,2,48,128]{3,2,1,0:T(8,128)(2,1)S(1)} %get-tuple-element.80), channel_id=1, source_target_pairs={{0,16},{16,32},{32,48},{48,0},{64,80},{80,96},{96,112},{112,64},{1... | collective-permute-start | bytes 294920 | tf_op jit(solution)/shard_map/ppermute | solution.py:295
  73.0 10.0 %collective-permute-start.14 = (bf16[4,2,48,128]{3,2,1,0:T(8,128)(2,1)S(1)}, bf16[4,2,48,128]{3,2,1,0:T(8,128)(2,1)S(1)}, u32[]{:S(2)}, u32[]{:S(2)}) collective-permute-start(bf16[4,2,48,128]{3,2,1,0:T(8,128)(2,1)S(1)} %get-tuple-element.84), channel_id=1, source_target_pairs={{0,32},{16,48},{32,0},{48,16},{64,96},{80,112},{96,64},{112,80},{1... | collective-permute-start | bytes 294920 | tf_op jit(solution)/shard_map/ppermute | solution.py:295
  73.0 10.0 %collective-permute-start.15 = (bf16[4,2,48,128]{3,2,1,0:T(8,128)(2,1)S(1)}, bf16[4,2,48,128]{3,2,1,0:T(8,128)(2,1)S(1)}, u32[]{:S(2)}, u32[]{:S(2)}) collective-permute-start(bf16[4,2,48,128]{3,2,1,0:T(8,128)(2,1)S(1)} %get-tuple-element.85), channel_id=1, source_target_pairs={{0,48},{16,0},{32,16},{48,32},{64,112},{80,64},{96,80},{112,96},{1... | collective-permute-start | bytes 294920 | tf_op jit(solution)/shard_map/ppermute | solution.py:295
  79.4 9.8 %collective-permute-start.16 = (bf16[1280,128]{1,0:T(8,128)(2,1)}, bf16[1280,128]{1,0:T(8,128)(2,1)S(1)}, u32[]{:S(2)}, u32[]{:S(2)}) collective-permute-start(bf16[1280,128]{1,0:T(8,128)(2,1)} %get-tuple-element.93), channel_id=1, source_target_pairs={{0,64},{16,80},{32,96},{48,112},{64,128},{80,144},{96,160},{112,17... | collective-permute-start | bytes 983048 | tf_op jit(solution)/shard_map/ppermute | solution.py:290
  82.3 8.5 %collective-permute-start.17 = (bf16[1280,128]{1,0:T(8,128)(2,1)}, bf16[1280,128]{1,0:T(8,128)(2,1)S(1)}, u32[]{:S(2)}, u32[]{:S(2)}) collective-permute-start(bf16[1280,128]{1,0:T(8,128)(2,1)} %get-tuple-element.94), channel_id=1, source_target_pairs={{0,192},{16,208},{32,224},{48,240},{64,0},{80,16},{96,32},{112,48}... | collective-permute-start | bytes 983048 | tf_op jit(solution)/shard_map/ppermute | solution.py:290
  83.1 29.1 %collective-permute-start.19 = (bf16[4,2,128,128]{3,2,1,0:T(8,128)(2,1)}, bf16[4,2,128,128]{3,2,1,0:T(8,128)(2,1)S(1)}, u32[]{:S(2)}, u32[]{:S(2)}) collective-permute-start(bf16[4,2,128,128]{3,2,1,0:T(8,128)(2,1)} %get-tuple-element.99), channel_id=1, source_target_pairs={{0,16},{16,32},{32,48},{48,0},{64,80},{80,96},{96,112},{112,64},{1... | collective-permute-start | bytes 786440 | tf_op jit(solution)/shard_map/ppermute | solution.py:295
  84.4 27.8 %collective-permute-start.20 = (bf16[4,2,128,128]{3,2,1,0:T(8,128)(2,1)}, bf16[4,2,128,128]{3,2,1,0:T(8,128)(2,1)S(1)}, u32[]{:S(2)}, u32[]{:S(2)}) collective-permute-start(bf16[4,2,128,128]{3,2,1,0:T(8,128)(2,1)} %get-tuple-element.100), channel_id=1, source_target_pairs={{0,32},{16,48},{32,0},{48,16},{64,96},{80,112},{96,64},{112,80},{1... | collective-permute-start | bytes 786440 | tf_op jit(solution)/shard_map/ppermute | solution.py:295
  86.3 25.9 %collective-permute-start.21 = (bf16[4,2,128,128]{3,2,1,0:T(8,128)(2,1)S(1)}, bf16[4,2,128,128]{3,2,1,0:T(8,128)(2,1)S(1)}, u32[]{:S(2)}, u32[]{:S(2)}) collective-permute-start(bf16[4,2,128,128]{3,2,1,0:T(8,128)(2,1)S(1)} %copy-done.6), channel_id=1, source_target_pairs={{0,48},{16,0},{32,16},{48,32},{64,112},{80,64},{96,80},{112,96},{1... | collective-permute-start | bytes 786440 | tf_op jit(solution)/shard_map/ppermute | solution.py:295
  90.8 22.1 %collective-permute-start.18 = (bf16[1280,128]{1,0:T(8,128)(2,1)S(1)}, bf16[1280,128]{1,0:T(8,128)(2,1)S(1)}, u32[]{:S(2)}, u32[]{:S(2)}) collective-permute-start(bf16[1280,128]{1,0:T(8,128)(2,1)S(1)} %copy-done.5), channel_id=1, source_target_pairs={{0,128},{16,144},{32,160},{48,176},{64,192},{80,208},{96,224},{112... | collective-permute-start | bytes 983048 | tf_op jit(solution)/shard_map/ppermute | solution.py:290
  90.8 21.4 %copy-start.1 = (bf16[4,2,128,128]{3,2,1,0:T(8,128)(2,1)S(1)}, bf16[4,2,128,128]{3,2,1,0:T(8,128)(2,1)}, u32[]{:S(2)}) copy-start(bf16[4,2,128,128]{3,2,1,0:T(8,128)(2,1)} %get-tuple-element.98.r0) | copy-start | bytes 786436
  90.9 1.4 %collective-permute-start = (bf16[2,192,128]{2,1,0:T(8,128)(2,1)S(1)}, bf16[2,192,128]{2,1,0:T(8,128)(2,1)S(1)}, u32[]{:S(2)}, u32[]{:S(2)}) collective-permute-start(bf16[2,192,128]{2,1,0:T(8,128)(2,1)S(1)} %convert_element_type.93), channel_id=1, source_target_pairs={{0,1},{1,0},{2,3},{3,2},{4,5},{5,4},{6,7},{7,6},{8,9},{9,8},{10,11... | collective-permute-start | bytes 294920 | tf_op jit(solution)/shard_map/while/body/ppermute | solution.py:299
  92.3 4.9 %collective-permute-start.1 = (bf16[2,192,128]{2,1,0:T(8,128)(2,1)S(1)}, bf16[2,192,128]{2,1,0:T(8,128)(2,1)S(1)}, u32[]{:S(2)}, u32[]{:S(2)}) collective-permute-start(bf16[2,192,128]{2,1,0:T(8,128)(2,1)S(1)} %add_convert_fusion.6), channel_id=1, source_target_pairs={{0,2},{1,3},{2,0},{3,1},{4,6},{5,7},{6,4},{7,5},{8,10},{9,11},{10,... | collective-permute-start | bytes 294920 | tf_op jit(solution)/shard_map/while/body/ppermute | solution.py:303
  97.3 6.2 %collective-permute-start.2 = (bf16[2,192,128]{2,1,0:T(8,128)(2,1)S(1)}, bf16[2,192,128]{2,1,0:T(8,128)(2,1)S(1)}, u32[]{:S(2)}, u32[]{:S(2)}) collective-permute-start(bf16[2,192,128]{2,1,0:T(8,128)(2,1)S(1)} %add_convert_fusion.7), channel_id=1, source_target_pairs={{0,4},{1,5},{2,6},{3,7},{4,0},{5,1},{6,2},{7,3},{8,12},{9,13},{10,... | collective-permute-start | bytes 294920 | tf_op jit(solution)/shard_map/while/body/ppermute | solution.py:303
  103.5 8.7 %collective-permute-start.3 = (bf16[2,192,128]{2,1,0:T(8,128)(2,1)S(1)}, bf16[2,192,128]{2,1,0:T(8,128)(2,1)S(1)}, u32[]{:S(2)}, u32[]{:S(2)}) collective-permute-start(bf16[2,192,128]{2,1,0:T(8,128)(2,1)S(1)} %add_convert_fusion.8), channel_id=1, source_target_pairs={{0,8},{1,9},{2,10},{3,11},{4,12},{5,13},{6,14},{7,15},{8,0},{9,1},... | collective-permute-start | bytes 294920 | tf_op jit(solution)/shard_map/while/body/ppermute | solution.py:307
  112.2 6.4 %copy-start = (bf16[1280,128]{1,0:T(8,128)(2,1)S(1)}, bf16[1280,128]{1,0:T(8,128)(2,1)}, u32[]{:S(2)}) copy-start(bf16[1280,128]{1,0:T(8,128)(2,1)} %get-tuple-element.78.d0) | copy-start | bytes 983044
  113.0 7.5 %collective-permute-start.22 = (bf16[352,128]{1,0:T(8,128)(2,1)S(1)}, bf16[352,128]{1,0:T(8,128)(2,1)S(1)}, u32[]{:S(2)}, u32[]{:S(2)}) collective-permute-start(bf16[352,128]{1,0:T(8,128)(2,1)S(1)} %get-tuple-element.114), channel_id=1, source_target_pairs={{0,64},{16,80},{32,96},{48,112},{64,128},{80,144},{96,160},{112,17... | collective-permute-start | bytes 270344 | tf_op jit(solution)/shard_map/ppermute | solution.py:290
  114.7 6.4 %collective-permute-start.23 = (bf16[352,128]{1,0:T(8,128)(2,1)S(1)}, bf16[352,128]{1,0:T(8,128)(2,1)S(1)}, u32[]{:S(2)}, u32[]{:S(2)}) collective-permute-start(bf16[352,128]{1,0:T(8,128)(2,1)S(1)} %get-tuple-element.115), channel_id=1, source_target_pairs={{0,128},{16,144},{32,160},{48,176},{64,192},{80,208},{96,224},{112... | collective-permute-start | bytes 270344 | tf_op jit(solution)/shard_map/ppermute | solution.py:290
  118.6 5.7 %collective-permute-start.24 = (bf16[352,128]{1,0:T(8,128)(2,1)S(1)}, bf16[352,128]{1,0:T(8,128)(2,1)S(1)}, u32[]{:S(2)}, u32[]{:S(2)}) collective-permute-start(bf16[352,128]{1,0:T(8,128)(2,1)S(1)} %get-tuple-element.116), channel_id=1, source_target_pairs={{0,192},{16,208},{32,224},{48,240},{64,0},{80,16},{96,32},{112,48}... | collective-permute-start | bytes 270344 | tf_op jit(solution)/shard_map/ppermute | solution.py:290
